TPU v7x, 128 devices: a whole 4x4x4 slice. The times are simulated.
128 devices in a mesh: group: 8 (over z, core), member: 16 (over y, x).
Axes of the slice: x: 4, y: 4, z: 4, core: 2. Of those that a mesh axis runs over, the one named last changes fastest.
Arguments:
- hist_row: int32 [128, 256], P(('group', 'member')), may hold values from 0 to 2047
- hist_owner: int32 [128, 256, 1], P(('group', 'member')), may hold values from 0 to 127; in each aligned block of 256 rows (0 to 255, 256 to 511, ..., all dimensions but the last counted through in order) at most 6 rows name the same one
- seq_len: int32 [128], P(('group', 'member')), may hold values from 128 to 256, as said below
- item_table: bfloat16 [262144, 512], P(('group', 'member')), may hold values from -6 to 6
- neg_rows: int32 [8, 8192], P('group', 'member'), may hold values from 0 to 2047
- in_weight: bfloat16 [512, 2048], replicated, may hold values from -0.25 to 0.25
- out_weight: bfloat16 [512, 512], replicated, may hold values from -0.25 to 0.25
Outputs:
- user_loss: float32 [128], P(('group', 'member'))
- in_grad: float32 [512, 2048], replicated
- out_grad: float32 [512, 512], replicated
- table_grad: float32 [262144, 512], P(('group', 'member'))
Inputs may be any that keep to these rules, and one draw needn't show every extreme that they name: `hist_owner`: no owner is named by more than 6 events of one user's history, a bound that some history reaches. `seq_len`: positions from a user's length on are padding; some user has the full length.
All inputs are finite; a program needn't handle non-finite values.
Results may differ from a plain program's by a relative error of at most 0.019.
Values may be sent and summed in bfloat16 or wider, within the bound.
No kernel may reach another device: no remote copies, remote signals or barrier semaphores. Data moves between devices by JAX's collectives and lax.ppermute only.
A program may use at most 128 MiB of HBM per device.

v0:
```python
import jax
import jax.numpy as jnp
from jax import lax
from jax.sharding import PartitionSpec as P

HEADS = 4


inverse_temp = 20.0


def layer_norm(values):
    average = jnp.mean(values, axis=-1, keepdims=True)
    centered = values - average
    return centered * lax.rsqrt(jnp.mean(centered * centered, axis=-1, keepdims=True) + 1e-05)


def hstu_layer(history, in_wide, out_wide, length):
    seqlen, model_width = history.shape
    head_size = model_width // HEADS
    normed = layer_norm(history).astype(jnp.bfloat16)
    hidden = jax.nn.silu(
        jnp.dot(normed, in_wide.astype(jnp.bfloat16), preferred_element_type=jnp.float32)
    ).astype(jnp.bfloat16)
    gate_cols = hidden[:, :model_width]
    value_cols = hidden[:, model_width : 2 * model_width].reshape(seqlen, HEADS, head_size)
    query_cols = hidden[:, 2 * model_width : 3 * model_width].reshape(seqlen, HEADS, head_size)
    key_cols = hidden[:, 3 * model_width :].reshape(seqlen, HEADS, head_size)
    scores = jnp.einsum(
        "qhd,khd->hqk", query_cols.astype(jnp.float32), key_cols.astype(jnp.float32)
    ) * head_size ** (-0.5)
    position = jnp.arange(seqlen)
    allowed = (position[None, :] <= position[:, None]) & (position[None, :] < length)
    attention = (
        jax.nn.silu(scores) * allowed[None].astype(jnp.float32) / length.astype(jnp.float32)
    ).astype(jnp.bfloat16)
    mixed_heads = jnp.einsum(
        "hqk,khd->qhd", attention.astype(jnp.float32), value_cols.astype(jnp.float32)
    ).reshape(seqlen, model_width)
    gated_out = (layer_norm(mixed_heads) * gate_cols.astype(jnp.float32)).astype(jnp.bfloat16)
    return (
        jnp.dot(gated_out, out_wide.astype(jnp.bfloat16), preferred_element_type=jnp.float32)
        + history
    )


def score_against(query_rows, neg_block):
    return inverse_temp * lax.dot_general(
        query_rows, neg_block, (((1,), (1,)), ((), ())), preferred_element_type=jnp.float32
    )


def local(hist_row, hist_owner, seq_len, item_table, neg_rows, in_weight, out_weight):
    devices = lax.axis_size(("group", "member"))
    wanted = hist_row[0]
    owners = hist_owner[0, :, 0]
    length = seq_len[0]
    seqlen = wanted.shape[0]
    model_width = item_table.shape[1]
    capacity = 3 * seqlen // devices
    onehot = (owners[:, None] == jnp.arange(devices, dtype=jnp.int32)[None, :]).astype(jnp.float32)
    position = jnp.arange(seqlen)
    earlier = (position[:, None] > position[None, :]).astype(jnp.float32)
    before = jnp.dot(earlier, onehot, precision=lax.Precision.HIGHEST)
    place_in = jnp.sum(before * onehot, axis=1).astype(jnp.int32)
    slots = owners * capacity + place_in
    requests = jnp.zeros((devices * capacity,), jnp.int32).at[slots].set(wanted)
    asked_rows = lax.all_to_all(
        requests.reshape(devices, capacity),
        ("group", "member"),
        split_axis=0,
        concat_axis=0,
        tiled=True,
    )
    found_rows = item_table[asked_rows]
    returned = lax.all_to_all(
        found_rows, ("group", "member"), split_axis=0, concat_axis=0, tiled=True
    )
    history = returned.reshape(devices * capacity, model_width)[slots].astype(jnp.float32)
    own_ids = neg_rows[0]
    own_rows = item_table[own_ids].astype(jnp.float32)
    own_scale = lax.rsqrt(jnp.sum(own_rows * own_rows, axis=-1, keepdims=True) + 1e-06)
    own_unit = own_rows * own_scale
    own_bf = own_unit.astype(jnp.bfloat16)
    in_wide = in_weight.astype(jnp.float32)
    out_wide = out_weight.astype(jnp.float32)
    output, pullback = jax.vjp(
        lambda first, second, third: hstu_layer(first, second, third, length),
        history,
        in_wide,
        out_wide,
    )
    query_scale = lax.rsqrt(jnp.sum(output * output, axis=-1, keepdims=True) + 1e-06)
    query_unit = output * query_scale
    query_bf = query_unit.astype(jnp.bfloat16)
    following = jnp.concatenate([history[1:], jnp.zeros_like(history[:1])], axis=0)
    pos_scale = lax.rsqrt(jnp.sum(following * following, axis=-1, keepdims=True) + 1e-06)
    pos_unit = following * pos_scale
    pos_score = inverse_temp * jnp.sum(query_unit * pos_unit, axis=-1)
    usable = (position < length - 1).astype(jnp.float32)
    negatives = lax.all_gather(own_bf, "member", axis=0, tiled=True)
    neg_score = score_against(query_bf, negatives)
    log_total = jnp.log(jnp.exp(pos_score) + jnp.sum(jnp.exp(neg_score), axis=-1))
    neg_weight = (inverse_temp * usable[:, None] * jnp.exp(neg_score - log_total[:, None])).astype(
        jnp.bfloat16
    )
    from_negs = jnp.dot(neg_weight, negatives, preferred_element_type=jnp.float32)
    neg_sum = lax.psum_scatter(
        lax.dot_general(
            neg_weight, query_bf, (((0,), (0,)), ((), ())), preferred_element_type=jnp.float32
        ).astype(jnp.bfloat16),
        "member",
        scatter_dimension=0,
        tiled=True,
    ).astype(jnp.float32)
    user_loss = jnp.sum((log_total - pos_score) * usable) / (length - 1).astype(jnp.float32)
    pos_grad = inverse_temp * usable * (jnp.exp(pos_score - log_total) - 1.0)
    own_grad = own_scale * (
        neg_sum - own_unit * jnp.sum(own_unit * neg_sum, axis=-1, keepdims=True)
    )
    query_grad = pos_grad[:, None] * pos_unit + from_negs
    output_grad = query_scale * (
        query_grad - query_unit * jnp.sum(query_unit * query_grad, axis=-1, keepdims=True)
    )
    unit_grad = pos_grad[:, None] * query_unit
    next_grad = pos_scale * (
        unit_grad - pos_unit * jnp.sum(pos_unit * unit_grad, axis=-1, keepdims=True)
    )
    shifted = jnp.concatenate([jnp.zeros_like(next_grad[:1]), next_grad[:-1]], axis=0)
    history_grad, in_part, out_part = pullback(output_grad)
    row_grad = history_grad + shifted
    outgoing = jnp.zeros((devices * capacity, model_width), jnp.float32).at[slots].set(row_grad)
    arrived = lax.all_to_all(
        outgoing.reshape(devices, capacity, model_width).astype(jnp.bfloat16),
        ("group", "member"),
        split_axis=0,
        concat_axis=0,
        tiled=True,
    ).astype(jnp.float32)
    table_grad = jnp.zeros((item_table.shape[0], model_width), jnp.float32)
    table_grad = table_grad.at[asked_rows.reshape(-1)].add(arrived.reshape(-1, model_width))
    table_grad = table_grad.at[own_ids].add(own_grad)
    in_grad, out_grad = lax.psum((in_part, out_part), ("group", "member"))
    return (user_loss.reshape(1), in_grad, out_grad, table_grad)


def solution(mesh):
    return jax.shard_map(
        local,
        mesh=mesh,
        in_specs=(
            P(("group", "member"), None),
            P(("group", "member"), None, None),
            P(("group", "member")),
            P(("group", "member"), None),
            P("group", "member"),
            P(),
            P(),
        ),
        out_specs=(P(("group", "member")), P(), P(), P(("group", "member"), None)),
        check_vma=False,
    )
```

profile of v0, /device:TPU:1, one launch (start us, length us, event | category | flops | bytes accessed | tf_op | source)
XLA Modules:
  0.0 377.5 jit_solution(2769320874480777793)
XLA Ops:
  8.1 3.8 %gather_fusion.2 = bf16[512,512]{1,0:T(8,128)(2,1)S(1)} fusion(bf16[2048,512]{1,0:T(8,128)(2,1)} %param.10, s32[1024]{0:T(1024)S(1)} %pad_clamp_fusion), kind=kCustom, calls=%fused_computation.2 | custom fusion | bytes 1050624 | tf_op jit(solution)/shard_map/gather | solution.py:81
  15.1 21.1 %all_to_all.22 = s32[128,1,6]{2,1,0:T(1,128)S(1)} all-to-all(s32[128,1,6]{2,1,0:T(1,128)S(1)} %bitcast.86), channel_id=1, replica_groups=mesh['group'=8,'member'=16] {'group','member'}, dimensions={0} | all-to-all | bytes 6144 | tf_op jit(solution)/shard_map/all_to_all | solution.py:68
  36.3 4.6 %gather_fusion = bf16[768,512]{1,0:T(8,128)(2,1)S(1)} fusion(bf16[2048,512]{1,0:T(8,128)(2,1)} %param.10, s32[1024]{0:T(1024)S(1)} %pad_clamp_fusion.2), kind=kCustom, calls=%fused_computation | custom fusion | bytes 1575936 | tf_op jit(solution)/shard_map/gather | solution.py:75
  42.2 5.2 %all-to-all-start.1 = ((bf16[128,6,512]{2,1,0:T(8,128)(2,1)}), bf16[128,6,512]{2,1,0:T(8,128)(2,1)}, u32[]{:S(2)}, u32[]{:S(2)}) async-start(bf16[128,6,512]{2,1,0:T(8,128)(2,1)} %reshape.319), calls=%async_computation.1 | async-start | bytes 2097152 | tf_op jit(solution)/shard_map/all_to_all | solution.py:76
  49.0 25.5 %all-to-all-done.1 = bf16[128,6,512]{2,1,0:T(8,128)(2,1)} async-done(((bf16[128,6,512]{2,1,0:T(8,128)(2,1)}), bf16[128,6,512]{2,1,0:T(8,128)(2,1)}, u32[]{:S(2)}, u32[]{:S(2)}) %all-to-all-start.1) | async-done | bytes 786464 | tf_op jit(solution)/shard_map/all_to_all | solution.py:76
  76.6 2.5 gather_fusion.1
  85.6 2.6 divide_convert_fusion
  96.5 5.0 %exponential_reduce_fusion = (f32[256]{0:T(256)S(1)}, f32[256,8192]{1,0:T(8,128)S(1)}) fusion(bf16[8192,512]{1,0:T(8,128)(2,1)} %all-gather.2.cloned.1.call-done, f32[256,512]{1,0:T(8,128)S(1)} %get-tuple-element.27, f32[256]{0:T(256)S(1)} %get-tuple-element.36), kind=kOutput, calls=%fused_computation.10 | convolution fusion | flops 2151939840 | bytes 17303552 | tf_op jit(solution)/shard_map/dot_general | solution.py:48
  102.2 2.5 copy-done.1
  104.7 5.4 %convolution_convert_fusion = bf16[8192,512]{1,0:T(8,128)(2,1)} fusion(f32[256,512]{1,0:T(8,128)S(1)} %get-tuple-element.27, f32[256]{0:T(256)S(1)} %get-tuple-element.36, f32[256,8192]{1,0:T(8,128)S(1)} %get-tuple-element.29, f32[256]{0:T(256)S(1)} %get-tuple-element.17, f32[256]{0:T(256)S(1)} %fusion.46), kind=kOutput, calls=%fused_computation.7 | convolution fusion | flops 2158231552 | bytes 17304576 | tf_op jit(solution)/shard_map/dot_general | solution.py:109
  110.5 9.2 %multiply_reduce_fusion = (f32[256]{0:T(256)S(1)}, f32[256,512]{1,0:T(8,128)}, f32[256]{0:T(256)S(1)}, f32[256,512]{1,0:T(8,128)S(1)}) fusion(f32[256,512]{1,0:T(8,128)} %get-tuple-element.11, f32[256,512]{1,0:T(8,128)S(1)} %get-tuple-element.27, f32[256]{0:T(256)S(1)} %get-tuple-element.36, f32[256]{0:T(256)S(1)} %get-tuple-element.19, ...), kind=kOutput, calls=%fused_computation.72 | convolution fusion | flops 2154823168 | bytes 18880512 | tf_op jit(solution)/shard_map/dot_general | solution.py:107
  128.9 2.1 fusion.21
  138.5 2.2 fusion.10
  140.8 5.3 %fusion = f32[512,2048]{1,0:T(8,128)} fusion(bf16[256,512]{1,0:T(8,128)(2,1)S(1)} %gather_fusion.1, f32[256]{0:T(256)S(1)} %fusion.47, f32[256]{0:T(256)S(1)} %broadcast_multiply_fusion.1, f32[256,2048]{1,0:T(8,128)} %get-tuple-element.21, bf16[256,512]{1,0:T(8,128)(2,1)} %get-tuple-element.12, bf16[256,512]{1,0:T(8,128)(2,1)} %copy.53, ...), kind=kOutput, calls=%fused_computation.13 | convolution fusion | flops 548405248 | bytes 7604224 | tf_op jit(solution)/shard_map/transpose(jvp())/dot_general | solution.py:23
  146.1 3.1 multiply_reduce_fusion.1
  151.4 3.6 scatter_custom_fusion.1
  157.7 7.8 %all-to-all-start.2 = ((bf16[128,6,512]{2,1,0:T(8,128)(2,1)}), bf16[128,6,512]{2,1,0:T(8,128)(2,1)}, u32[]{:S(2)}, u32[]{:S(2)}) async-start(bf16[128,6,512]{2,1,0:T(8,128)(2,1)} %convert_element_type.170), calls=%async_computation.2 | async-start | bytes 2097152 | tf_op jit(solution)/shard_map/all_to_all | solution.py:133
  167.7 17.1 %all-to-all-done.2 = bf16[128,6,512]{2,1,0:T(8,128)(2,1)} async-done(((bf16[128,6,512]{2,1,0:T(8,128)(2,1)}), bf16[128,6,512]{2,1,0:T(8,128)(2,1)}, u32[]{:S(2)}, u32[]{:S(2)}) %all-to-all-start.2) | async-done | bytes 786464 | tf_op jit(solution)/shard_map/all_to_all | solution.py:133
  184.8 2.4 reshape.362
  187.2 9.5 %scatter_custom_fusion.2 = f32[2048,512]{1,0:T(8,128)} fusion(s32[768]{0:T(1024)S(1)} %fusion.43, f32[768,512]{1,0:T(8,128)} %reshape.362, f32[]{:T(128)} %constant.19.clone.1), kind=kCustom, calls=%fused_computation.18 | custom fusion | flops 393216 | bytes 4194816 | tf_op jit(solution)/shard_map/scatter-add | solution.py:141
  196.7 4.7 %reduce-scatter.2.cloned.1.call-done = bf16[512,512]{1,0:T(8,128)(2,1)} async-done(((bf16[8192,512]{1,0:T(8,128)(2,1)}), bf16[512,512]{1,0:T(8,128)(2,1)}) %reduce-scatter.2.cloned.1.call-update) | async-done | bytes 524304 | tf_op jit(solution)/shard_map/reduce_scatter | solution.py:108
  202.8 8.5 %scatter_custom_fusion.3 = f32[2048,512]{1,0:T(8,128)} fusion(f32[2048,512]{1,0:T(8,128)} %scatter_custom_fusion.2, s32[512]{0:T(512)S(1)} %bitcast.89, bf16[512,512]{1,0:T(8,128)(2,1)S(1)} %gather_fusion.2, bf16[512,512]{1,0:T(8,128)(2,1)} %reduce-scatter.2.cloned.1.call-done, f32[512]{0:T(512)S(1)} %fusion.15, f32[512]{0:T(512)S(1)} %add_rsqrt_fusion), kind=kCustom, calls=%fused_computation.50 | custom fusion | flops 1835008 | bytes 5246976 | tf_op jit(solution)/shard_map/scatter-add | solution.py:142
  211.3 152.8 %all-reduce.9.cloned.1.call-done = (f32[512,2048]{1,0:T(8,128)}, f32[512,512]{1,0:T(8,128)}) async-done(((f32[512,2048]{1,0:T(8,128)}, f32[512,512]{1,0:T(8,128)}), (f32[512,2048]{1,0:T(8,128)}, f32[512,512]{1,0:T(8,128)})) %all-reduce.9.cloned.1.call-update) | async-done | bytes 5242896 | tf_op jit(solution)/shard_map/psum | solution.py:143
  364.1 4.8 %copy.71 = f32[512,2048]{1,0:T(8,128)} copy(f32[512,2048]{1,0:T(8,128)} %get-tuple-element.38) | data formatting | bytes 8388608
  (114 shorter events, 49.4 us)
Async XLA Ops:
  7.2 73.2 %copy-start = (bf16[512,2048]{1,0:T(8,128)(2,1)S(1)}, bf16[512,2048]{1,0:T(8,128)(2,1)}, u32[]{:S(2)}) copy-start(bf16[512,2048]{1,0:T(8,128)(2,1)} %param.12) | copy-start | bytes 6291460
  7.2 89.3 %all-gather.2.cloned.1.call-start = ((), (), s32[]{:S(2)}) async-start(), calls=%async_computation.4 | async-start | bytes 8912896 | tf_op jit(solution)/shard_map/all_gather | solution.py:101
  11.9 1.2 copy-start.21
  42.2 32.3 %all-to-all-start.1 = ((bf16[128,6,512]{2,1,0:T(8,128)(2,1)}), bf16[128,6,512]{2,1,0:T(8,128)(2,1)}, u32[]{:S(2)}, u32[]{:S(2)}) async-start(bf16[128,6,512]{2,1,0:T(8,128)(2,1)} %reshape.319), calls=%async_computation.1 | async-start | bytes 2097152 | tf_op jit(solution)/shard_map/all_to_all | solution.py:76
  47.4 154.0 %reduce-scatter.2.cloned.1.call-start = ((), (), s32[]{:S(2)}) async-start(), calls=%async_computation.5 | async-start | bytes 8912896 | tf_op jit(solution)/shard_map/reduce_scatter | solution.py:108
  82.4 1.0 copy-start.7
  84.4 3.8 %copy-start.16 = (bf16[256,512]{0,1:T(8,128)(2,1)}, bf16[256,512]{0,1:T(8,128)(2,1)S(1)}, u32[]{:S(2)}) copy-start(bf16[256,512]{0,1:T(8,128)(2,1)S(1)} %copy.55) | copy-start | bytes 786436
  85.6 2.6 copy-start.17
  85.6 2.6 copy-start.19
  88.2 1.1 copy-start.11
  90.6 2.6 copy-start.3
  90.6 4.4 %copy-start.13 = (bf16[512,512]{1,0:T(8,128)(2,1)S(1)}, bf16[512,512]{1,0:T(8,128)(2,1)}, u32[]{:S(2)}) copy-start(bf16[512,512]{1,0:T(8,128)(2,1)} %param.13) | copy-start | bytes 1572868
  90.6 4.8 %copy-start.5 = (f32[255,512]{1,0:T(8,128)S(1)}, f32[255,512]{1,0:T(8,128)}, u32[]{:S(2)}) copy-start(f32[255,512]{1,0:T(8,128)} %slice.34) | copy-start | bytes 1566724
  95.4 15.1 %copy-start.2 = (f32[256,512]{1,0:T(8,128)}, f32[256,512]{1,0:T(8,128)S(1)}, u32[]{:S(2)}) copy-start(f32[256,512]{1,0:T(8,128)S(1)} %get-tuple-element.27) | copy-start | bytes 1572868
  101.5 3.2 copy-start.1
  110.2 253.9 %all-reduce.9.cloned.1.call-start = ((), (), s32[]{:S(2)}) async-start(), calls=%async_computation.6 | async-start | bytes 10485760 | tf_op jit(solution)/shard_map/psum | solution.py:143
  110.5 10.4 %copy-start.4 = (f32[256,512]{1,0:T(8,128)S(1)}, f32[256,512]{1,0:T(8,128)}, u32[]{:S(2)}) copy-start(f32[256,512]{1,0:T(8,128)} %copy-done.3) | copy-start | bytes 1572868
  110.5 10.4 %copy-start.8 = (bf16[256,2048]{1,0:T(8,128)(2,1)S(1)}, bf16[256,2048]{1,0:T(8,128)(2,1)}, u32[]{:S(2)}) copy-start(bf16[256,2048]{1,0:T(8,128)(2,1)} %copy-done.7) | copy-start | bytes 3145732
  110.5 10.4 %copy-start.14 = (bf16[512,512]{1,0:T(8,128)(2,1)S(1)}, bf16[512,512]{1,0:T(8,128)(2,1)}, u32[]{:S(2)}) copy-start(bf16[512,512]{1,0:T(8,128)(2,1)} %param.13) | copy-start | bytes 1572868
  128.9 3.0 copy-start.18
  146.1 4.2 %copy-start.10 = (f32[256,512]{1,0:T(8,128)S(1)}, f32[256,512]{1,0:T(8,128)}, u32[]{:S(2)}) copy-start(f32[256,512]{1,0:T(8,128)} %get-tuple-element.11) | copy-start | bytes 1572868
  146.1 4.2 %copy-start.20 = (f32[256,512]{1,0:T(8,128)S(1)}, f32[256,512]{1,0:T(8,128)}, u32[]{:S(2)}) copy-start(f32[256,512]{1,0:T(8,128)} %get-tuple-element.7) | copy-start | bytes 1572868
  157.7 27.1 %all-to-all-start.2 = ((bf16[128,6,512]{2,1,0:T(8,128)(2,1)}), bf16[128,6,512]{2,1,0:T(8,128)(2,1)}, u32[]{:S(2)}, u32[]{:S(2)}) async-start(bf16[128,6,512]{2,1,0:T(8,128)(2,1)} %convert_element_type.170), calls=%async_computation.2 | async-start | bytes 2097152 | tf_op jit(solution)/shard_map/all_to_all | solution.py:133
  364.1 4.8 %copy-start.15 = (f32[512,512]{1,0:T(8,128)S(1)}, f32[512,512]{1,0:T(8,128)}, u32[]{:S(2)}) copy-start(f32[512,512]{1,0:T(8,128)} %get-tuple-element.39) | copy-start | bytes 3145732
  (3 other events, 2.3 us)
Sparse Core Ops, SparseCore 0:
  13.2 82.5 all-gather.1
  110.3 91.0 reduce-scatter.1
  207.2 156.8 all-reduce.8
where the time goes:
time: 379 us; the launch traced here: 378 us
  waiting for transfers between devices  200 us (53%)
  matrix products  44.5 us (12%)
  local copies, waits for them, and re-layouts  43.5 us (11%)
  other arithmetic  38 us (10%)
  blocking collectives  21.1 us (6%)
  between operations  16.7 us (4%)
  starting transfers between devices  13.5 us (4%)
    psum x1, waiting for transfers between devices, local(): in_grad, out_grad = lax.psum((in_part, out_part), ('group', 'member'))  153 us
    all_to_all x1, waiting for transfers between devices, local(): lax.all_to_all(found_rows, ('group', 'member'), split_axis=0, concat_axis...  25.5 us
    all_to_all x1, blocking collectives, local(): lax.all_to_all(requests.reshape(devices, capacity), ('group', 'member'),...  21.1 us
    all_to_all x1, waiting for transfers between devices, local(): lax.all_to_all(outgoing.reshape(devices, capacity, model_width).astype(jn...  17.1 us
    unnamed x47, local copies, waits for them, and re-layouts  12.4 us
    dot_general x3, matrix products, hstu_layer(): jnp.dot(normed, in_wide.astype(jnp.bfloat16), preferred_element_type=jnp....  10.5 us
    scatter-add x1, other arithmetic, local(): table_grad.at[asked_rows.reshape(-1)].add(arrived.reshape(-1, model_width))  9.51 us
    dot_general x1, matrix products, local(): jnp.dot(neg_weight, negatives, preferred_element_type=jnp.float32)  9.15 us
  transfers between devices with their start and end apart: 5, of which 4 were waited for; matrix products, arithmetic and copies ran while one was open for 26% of the time, Pallas kernels for 0%

commit v1 on v0

v1 whole, which is shorter than its diff:
```python
import functools
import jax
import jax.numpy as jnp
from jax import lax
from jax.experimental import pallas as pl
from jax.experimental.pallas import tpu as pltpu
from jax.sharding import PartitionSpec as P

HEADS = 4
SLOTS = 8
SIDE = 4
TEMP = 20.0
BF = jnp.bfloat16
F32 = jnp.float32
AXES = ("group", "member")
MIB = 1024 * 1024


def mm(a, b):
    return jnp.dot(a, b, preferred_element_type=F32)


def mm_nt(a, b):
    return lax.dot_general(a, b, (((1,), (1,)), ((), ())), preferred_element_type=F32)


def mm_tn(a, b):
    return lax.dot_general(a, b, (((0,), (0,)), ((), ())), preferred_element_type=F32)


def iota(shape, dim):
    return lax.broadcasted_iota(jnp.int32, shape, dim)


def ones_where(mask):
    return jnp.where(mask, 1.0, 0.0).astype(BF)


def sigmoid(v):
    return 0.5 * jnp.tanh(0.5 * v) + 0.5


def norm_parts(values):
    centered = values - jnp.mean(values, axis=-1, keepdims=True)
    scale = lax.rsqrt(jnp.mean(centered * centered, axis=-1, keepdims=True) + 1e-05)
    return centered * scale, scale


def norm_back(unit, scale, grad):
    return scale * (
        grad
        - jnp.mean(grad, axis=-1, keepdims=True)
        - unit * jnp.mean(grad * unit, axis=-1, keepdims=True)
    )


def row_to_col(row):
    size = row.shape[1]
    eye = iota((128, 128), 0) == iota((128, 128), 1)
    parts = [
        jnp.sum(jnp.where(eye, row[:, k : k + 128], 0), axis=1, keepdims=True)
        for k in range(0, size, 128)
    ]
    return jnp.concatenate(parts, axis=0)


def col_to_rows(col):
    return jnp.transpose(jnp.broadcast_to(col, (col.shape[0], 128)))[:8]


class Fetched:
    def __init__(self, source, here, sem):
        self.here, self.shape, self.waited = here, here.shape, False
        self.copy = pltpu.make_async_copy(source, here, sem)
        self.copy.start()

    def __getitem__(self, index):
        if not self.waited:
            self.copy.wait()
            self.waited = True
        return self.here[index]


class Sent:
    def __init__(self, target, here, sems):
        self.target, self.here, self.sems, self.copies = target, here, sems, []
        self.shape, self.dtype = here.shape, here.dtype

    def __getitem__(self, index):
        return self.here[index]

    def __setitem__(self, index, value):
        self.here[index] = value
        if index is Ellipsis:
            source, target = self.here, self.target
        else:
            source, target = self.here.at[index], self.target.at[index]
        copy = pltpu.make_async_copy(source, target, self.sems.at[len(self.copies)])
        copy.start()
        self.copies.append(copy)


PARTS = 8
FAR = False


def call(
    kernel, outs, *args, smem=(), far=(), far_out=(), flops=0, name=None, scratch=(), after=(), vmem=40
):
    if not FAR:
        far, far_out = (), ()
    in_specs = [
        pl.BlockSpec(memory_space=pltpu.SMEM if i in smem else pl.ANY if i in far else pltpu.VMEM)
        for i in range(len(args))
    ] + [pl.BlockSpec(memory_space=pl.ANY)] * len(after)
    given, late, shown = len(args), len(after), len(outs)
    hidden = [pltpu.VMEM(args[i].shape, args[i].dtype) for i in far]
    hidden += [pltpu.VMEM(outs[i].shape, outs[i].dtype) for i in far_out]
    hidden += [pltpu.SemaphoreType.DMA((len(far) + 1,))]
    hidden += [pltpu.SemaphoreType.DMA((PARTS,)) for _ in far_out]

    def body(*refs):
        ins, results = list(refs[:given]), list(refs[given + late : given + late + shown])
        rest = refs[given + late + shown :]
        own, rest = rest[: len(scratch)], rest[len(scratch) :]
        sems = rest[len(far) + len(far_out)]
        for n, i in enumerate(far):
            ins[i] = Fetched(ins[i], rest[n], sems.at[n])
        sent = []
        for n, i in enumerate(far_out):
            results[i] = Sent(results[i], rest[len(far) + n], rest[len(far) + len(far_out) + 1 + n])
            sent.append(results[i])
        kernel(*ins, *results, *own)
        for result in sent:
            for copy in result.copies:
                copy.wait()

    moved = sum(a.size * a.dtype.itemsize for a in args)
    moved += sum(o.size * o.dtype.itemsize for o in outs)
    return pl.pallas_call(
        body,
        out_shape=outs,
        in_specs=in_specs,
        out_specs=[
            pl.BlockSpec(memory_space=pltpu.HBM if i in far_out else pltpu.VMEM)
            for i in range(len(outs))
        ],
        scratch_shapes=list(scratch) + hidden,
        compiler_params=pltpu.CompilerParams(vmem_limit_bytes=vmem * MIB),
        cost_estimate=pl.CostEstimate(flops=flops, bytes_accessed=moved, transcendentals=0),
        name=name,
    )(*args, *after)


def out(shape, dtype):
    return jax.ShapeDtypeStruct(shape, dtype)


def slots_kernel(owner_ref, row_ref, slots_ref, req_ref):
    owner = row_to_col(owner_ref[...])
    seqlen = owner.shape[0]
    devices = req_ref.shape[0]
    named = ones_where(owner == iota((seqlen, devices), 1))
    earlier = ones_where(iota((seqlen, seqlen), 0) > iota((seqlen, seqlen), 1))
    before = mm(earlier, named)
    place = jnp.sum(before * named.astype(F32), axis=1, keepdims=True).astype(jnp.int32)
    slots_ref[...] = owner * SLOTS + place
    wanted = row_to_col(row_ref[...])
    at_place = iota((seqlen, 128), 1) == place
    high = jnp.where(at_place, wanted >> 6, 0).astype(F32).astype(BF)
    low = jnp.where(at_place, wanted & 63, 0).astype(F32).astype(BF)
    asked = mm_tn(named, high) * 64.0 + mm_tn(named, low)
    req_ref[...] = asked[:, :SLOTS].astype(jnp.int32)


def find_kernel(asked_ref, table_ref, found_ref):
    asked = asked_ref[...]
    devices = asked.shape[0]
    rows = table_ref.shape[0]
    block = 256
    high = (asked >> 6).astype(F32).astype(BF)
    low = (asked & 63).astype(F32).astype(BF)
    for k in range(0, devices * SLOTS, block):
        spread = ones_where(
            (iota((block, devices), 0) + k) // SLOTS == iota((block, devices), 1)
        )
        every = mm(spread, high) * 64.0 + mm(spread, low)
        mine = (iota((block, SLOTS), 0) & (SLOTS - 1)) == iota((block, SLOTS), 1)
        ids = jnp.sum(jnp.where(mine, every, 0.0), axis=1, keepdims=True).astype(jnp.int32)
        pick = ones_where(ids == iota((block, rows), 1))
        found_ref[k : k + block, :] = mm(pick, table_ref[...]).astype(BF)


def own_kernel(ids_ref, table_ref, rows_ref, unit_ref):
    ids = row_to_col(ids_ref[...])
    rows = table_ref.shape[0]
    block = 256
    for k in range(0, ids.shape[0], block):
        pick = ones_where(ids[k : k + block] == iota((block, rows), 1))
        got = mm(pick, table_ref[...])
        rows_ref[k : k + block, :] = got.astype(BF)
        scale = lax.rsqrt(jnp.sum(got * got, axis=-1, keepdims=True) + 1e-06)
        unit_ref[k : k + block, :] = (got * scale).astype(BF)


def attention_of(query, key, length):
    seqlen, head_size = query.shape
    scores = mm_nt(query, key) * head_size ** (-0.5)
    at, of = iota((seqlen, seqlen), 0), iota((seqlen, seqlen), 1)
    allowed = (of <= at) & (of < length)
    share = jnp.where(allowed, 1.0 / length.astype(F32), 0.0)
    return scores, share


def following_of(history):
    seqlen = history.shape[0]
    moved = pltpu.roll(history, seqlen - 1, 0)
    return jnp.where(iota(history.shape, 0) < seqlen - 1, moved, 0.0)


def layer(length, history, in_ref, out_ref, mixed_ref, pre_ref=None):
    width = history.shape[1]
    head = width // HEADS
    normed = norm_parts(history.astype(F32))[0].astype(BF)
    parts = []
    for k in range(4):
        pre = mm(normed, in_ref[:, k * width : (k + 1) * width])
        if pre_ref is not None:
            pre_ref[:, k * width : (k + 1) * width] = pre
        parts.append((pre * sigmoid(pre)).astype(BF))
    gate, values, queries, keys = parts
    for h in range(HEADS):
        cols = slice(h * head, (h + 1) * head)
        scores, share = attention_of(queries[:, cols], keys[:, cols], length)
        attention = (scores * sigmoid(scores) * share).astype(BF)
        mixed_ref[:, cols] = mm(attention, values[:, cols])
    gated = (norm_parts(mixed_ref[...])[0] * gate.astype(F32)).astype(BF)
    return mm(gated, out_ref[...]) + history.astype(F32)


def forward_kernel(
    len_ref, back_ref, slots_ref, in_ref, out_ref, hist_ref, query_ref, pos_ref, mixed_ref
):
    seqlen = hist_ref.shape[0]
    length = len_ref[0]
    pick = ones_where(slots_ref[...] == iota((seqlen, back_ref.shape[0]), 1))
    hist_ref[...] = mm(pick, back_ref[...]).astype(BF)
    output = layer(length, hist_ref[...], in_ref, out_ref, mixed_ref)
    scale = lax.rsqrt(jnp.sum(output * output, axis=-1, keepdims=True) + 1e-06)
    query_unit = output * scale
    query_ref[...] = query_unit.astype(BF)
    following = following_of(hist_ref[...].astype(F32))
    pos_scale = lax.rsqrt(jnp.sum(following * following, axis=-1, keepdims=True) + 1e-06)
    pos_score = TEMP * jnp.sum(query_unit * (following * pos_scale), axis=-1, keepdims=True)
    rows = col_to_rows(pos_score)
    usable = jnp.where(iota(rows.shape, 1) < length - 1, 1.0, 0.0)
    pos_ref[...] = jnp.where(iota(rows.shape, 0) == 0, rows, usable)


def again_kernel(len_ref, hist_ref, in_ref, out_ref, pre_ref, mixed_ref, output_ref):
    output_ref[...] = layer(len_ref[0], hist_ref[...], in_ref, out_ref, mixed_ref, pre_ref)


def scores_kernel(count, query_ref, *refs):
    negs, others = refs[:SIDE], refs[SIDE : SIDE + count]
    weights_ref, grad_ref, total_ref = refs[-3:]
    query = query_ref[...]
    total = jnp.zeros((query.shape[0], 1), F32)
    grad = jnp.zeros(query.shape, F32)
    for k, neg_ref in enumerate(negs):
        neg = neg_ref[...]
        size = neg.shape[0]
        weight = jnp.exp(TEMP * mm_nt(query, neg))
        total = total + jnp.sum(weight, axis=1, keepdims=True)
        weight = weight.astype(BF)
        weights_ref[:, k * size : (k + 1) * size] = weight
        grad = grad + mm(weight, neg)
    grad_ref[...] = grad.astype(grad_ref.dtype)
    total = col_to_rows(total)
    row = iota(total.shape, 0)
    for k, ref in enumerate(others[:-1]):
        total = jnp.where(row == k, ref[...], total)
    if others:
        total = jnp.where(row == SIDE, others[-1][0:1, :], total)
        total = jnp.where(row == SIDE + 1, others[-1][1:2, :], total)
    total_ref[...] = total


def row_to_f32_col(row):
    return jnp.transpose(jnp.broadcast_to(row, (128, row.shape[1])))[:, 0:1]


def neg_kernel(len_ref, *refs):
    packs, queries, weights = refs[:SIDE], refs[SIDE : 2 * SIDE], refs[2 * SIDE : 3 * SIDE]
    outs, (loss_ref, factor_ref) = refs[3 * SIDE : -2], refs[-2:]
    scaled = []
    for k, query_ref in enumerate(queries):
        pos_score, usable = packs[k][SIDE : SIDE + 1, :], packs[k][SIDE + 1 : SIDE + 2, :]
        total = jnp.exp(pos_score)
        for j, ref in enumerate(packs):
            total = total + ref[j ^ k : (j ^ k) + 1, :]
        log_total = jnp.log(total)
        if k == 0:
            loss = jnp.sum((log_total - pos_score) * usable, axis=1, keepdims=True)
            loss_ref[...] = loss / (len_ref[0] - 1).astype(F32)
        factor = row_to_f32_col(TEMP * usable * jnp.exp(-log_total))
        if k == 0:
            factor_ref[...] = factor
        scaled.append((query_ref[...].astype(F32) * factor).astype(BF))
    for k, ref in enumerate(outs):
        size = ref.shape[0]
        cols = slice(k * size, (k + 1) * size)
        total = mm_tn(weights[0][:, cols], scaled[0])
        for w, q in zip(weights[1:], scaled[1:]):
            total = total + mm_tn(w[:, cols], q)
        ref[...] = total.astype(ref.dtype)


def backward_kernel(
    len_ref, at_ref, factor_ref, sum0, sum1, sum2, sum3, hist_ref, pre_ref, mixed_ref, output_ref,
    in_ref, out_ref,
    row_ref, keep_ref, send_ref,
    normed_ref, gated_ref, dpre_ref,
):
    length = len_ref[0]
    core = at_ref[3]
    seqlen, width = hist_ref.shape
    head = width // HEADS
    history = hist_ref[...].astype(F32)
    output = output_ref[...]
    query_scale = lax.rsqrt(jnp.sum(output * output, axis=-1, keepdims=True) + 1e-06)
    query_unit = output * query_scale
    following = following_of(history)
    pos_scale = lax.rsqrt(jnp.sum(following * following, axis=-1, keepdims=True) + 1e-06)
    pos_unit = following * pos_scale
    pos_score = TEMP * jnp.sum(query_unit * pos_unit, axis=-1, keepdims=True)
    from_negs = jnp.zeros((seqlen, width), F32)
    for ref in (sum0, sum1, sum2, sum3):
        from_negs = from_negs + ref[...].astype(F32)
    usable = jnp.where(iota((seqlen, 1), 0) < length - 1, 1.0, 0.0)
    factor = factor_ref[...]
    pos_grad = factor * jnp.exp(pos_score) - TEMP * usable
    query_grad = pos_grad * pos_unit + factor * from_negs
    output_grad = query_scale * (
        query_grad - query_unit * jnp.sum(query_unit * query_grad, axis=-1, keepdims=True)
    )
    unit_grad = pos_grad * query_unit
    next_grad = pos_scale * (
        unit_grad - pos_unit * jnp.sum(pos_unit * unit_grad, axis=-1, keepdims=True)
    )
    shifted = jnp.where(iota((seqlen, width), 0) > 0, pltpu.roll(next_grad, 1, 0), 0.0)

    def hidden_of(k):
        pre = pre_ref[:, k * width : (k + 1) * width]
        return (pre * sigmoid(pre)).astype(BF)

    def store(k, cols, grad):
        cols = slice(k * width + cols.start, k * width + cols.stop)
        pre = pre_ref[:, cols]
        s = sigmoid(pre)
        grad = grad.astype(BF).astype(F32) * (s * (1.0 + pre * (1.0 - s)))
        dpre_ref[:, cols] = grad.astype(BF)

    gate = hidden_of(0).astype(F32)
    mixed_unit, mixed_scale = norm_parts(mixed_ref[...])
    gated_ref[...] = (mixed_unit * gate).astype(BF)
    output_bf = output_grad.astype(BF)
    d_gated = mm_nt(output_bf, out_ref[...]).astype(BF).astype(F32)
    store(0, slice(0, width), d_gated * mixed_unit)
    d_mixed = norm_back(mixed_unit, mixed_scale, d_gated * gate).astype(BF)
    values, queries, keys = hidden_of(1), hidden_of(2), hidden_of(3)
    for h in range(HEADS):
        cols = slice(h * head, (h + 1) * head)
        q, k, v, d = queries[:, cols], keys[:, cols], values[:, cols], d_mixed[:, cols]
        scores, share = attention_of(q, k, length)
        s = sigmoid(scores)
        attention = (scores * s * share).astype(BF)
        d_attention = mm_nt(d, v).astype(BF).astype(F32)
        d_scores = d_attention * share * (s * (1.0 + scores * (1.0 - s)))
        d_scores = (d_scores * head ** (-0.5)).astype(BF)
        store(1, cols, mm_tn(attention, d))
        store(2, cols, mm(d_scores, k))
        store(3, cols, mm_tn(d_scores, q))
    normed, scale = norm_parts(history)
    normed_ref[...] = normed.astype(BF)
    half = width // 2
    for ref, which in ((send_ref, 1 - core), (keep_ref, core)):
        rows = pl.ds(pl.multiple_of(which * half, half), half)
        mine = normed_ref[:, rows]
        for k in range(4):
            cols = slice(k * width, (k + 1) * width)
            ref[:, cols] = mm_tn(mine, dpre_ref[:, cols]).astype(BF)
        ref[:, 4 * width :] = mm_tn(gated_ref[:, rows], output_bf).astype(BF)
    d_normed = mm_nt(dpre_ref[...], in_ref[...]).astype(BF).astype(F32)
    row_ref[...] = (output_grad + norm_back(normed, scale, d_normed) + shifted).astype(BF)


def going_kernel(slots_ref, row_ref, going_ref):
    pick = ones_where(slots_ref[...] == iota((row_ref.shape[0], going_ref.shape[0]), 1))
    going_ref[...] = mm_tn(pick, row_ref[...]).astype(BF)


def table_kernel(
    asked_ref, arrived_ref, ids_ref, rows_ref, neg0, neg1, neg2, neg3, table_ref, grad_ref
):
    block = table_ref.shape[0]

    @pl.when(pl.program_id(0) == 0)
    def _():
        rows = rows_ref[...].astype(F32)
        scale = lax.rsqrt(jnp.sum(rows * rows, axis=-1, keepdims=True) + 1e-06)
        unit = rows * scale
        total = neg0[...] + neg1[...].astype(F32) + neg2[...].astype(F32) + neg3[...].astype(F32)
        grad = scale * (total - unit * jnp.sum(unit * total, axis=-1, keepdims=True))
        grad_ref[...] = grad.astype(BF)

    first = pl.program_id(0) * block
    asked, ids = asked_ref[...], ids_ref[...]
    pick = ones_where(asked == iota((block, asked.shape[1]), 0) + first)
    total = mm(pick, arrived_ref[...])
    pick = ones_where(ids == iota((block, ids.shape[1]), 0) + first)
    table_ref[...] = total + mm(pick, grad_ref[...])


def table_grad_of(asked, arrived, ids, rows, negs, owned):
    width = arrived.shape[1]
    block = 512
    whole = pl.BlockSpec(memory_space=pltpu.VMEM)
    return pl.pallas_call(
        table_kernel,
        grid=(owned // block,),
        out_shape=out((owned, width), F32),
        in_specs=[whole] * 8,
        out_specs=pl.BlockSpec((block, width), lambda i: (i, 0)),
        scratch_shapes=[pltpu.VMEM(rows.shape, BF)],
        compiler_params=pltpu.CompilerParams(vmem_limit_bytes=40 * MIB),
        cost_estimate=pl.CostEstimate(
            flops=2 * owned * (arrived.shape[0] + rows.shape[0]) * width,
            bytes_accessed=owned * width * 4,
            transcendentals=0,
        ),
        name="table_grad",
    )(asked, arrived, ids, rows, *negs)


def quarters(at_ref, place, total_ref, outs):
    me = at_ref[place]
    for s, ref in enumerate(outs):
        size = ref.shape[0]
        which = (me + s) & (SIDE - 1)
        part = total_ref[pl.ds(pl.multiple_of(which * size, size), size), :]
        ref[...] = part.astype(ref.dtype)


def sum_of(refs):
    total = refs[0][...].astype(F32)
    for ref in refs[1:]:
        total = total + ref[...].astype(F32)
    return total


def scatter_kernel(place, count, at_ref, *refs):
    ins, outs, total_ref = refs[:count], refs[count:-1], refs[-1]
    total_ref[...] = sum_of(ins)
    quarters(at_ref, place, total_ref, outs)


def last_kernel(*refs):
    refs[-1][...] = sum_of(refs[:-1]).astype(refs[-1].dtype)


def total_kernel(p0, p1, p2, p3, total_ref):
    even = p0[...].astype(F32) + p2[...].astype(F32)
    odd = p1[...].astype(F32) + p3[...].astype(F32)
    total_ref[...] = (even + odd).astype(total_ref.dtype)


def stack_kernel(*refs):
    size = refs[0].shape[0]
    for k, ref in enumerate(refs[:-1]):
        refs[-1][k * size : (k + 1) * size] = ref[...]


def place_kernel(at_ref, mine_ref, other_ref, in_ref, out_ref):
    y, z, core = at_ref[1], at_ref[2], at_ref[3]
    count, rows, cols = mine_ref.shape
    half, width = in_ref.shape[0] // 2, in_ref.shape[1]
    for which, ref in ((core, mine_ref), (1 - core, other_ref)):
        for i in range(count):
            row = which * half + ((z - i // SIDE) & 3) * (half // SIDE)
            row = row + ((y - i % SIDE) & 3) * rows
            place = pl.ds(pl.multiple_of(row, rows), rows)
            part = ref[i].astype(F32)
            in_ref[place, :] = part[:, :width]
            out_ref[place, :] = part[:, width:]


def moves(axis, shift):
    if axis == "z":
        return "group", [(z * 2 + c, (z + shift) % SIDE * 2 + c) for z in range(SIDE) for c in range(2)]
    if axis == "core":
        return "group", [(g, g ^ 1) for g in range(2 * SIDE)]
    pairs = [(y, x) for y in range(SIDE) for x in range(SIDE)]
    if axis == "x":
        return "member", [(y * SIDE + x, y * SIDE + (x + shift) % SIDE) for y, x in pairs]
    return "member", [(y * SIDE + x, (y + shift) % SIDE * SIDE + x) for y, x in pairs]


def shift_by(value, axis, shift):
    name, pairs = moves(axis, shift)
    return lax.ppermute(value, name, pairs)


def spread(value, axis):
    return [value] + [shift_by(value, axis, s) for s in range(1, SIDE)]


def across(value, kind):
    step = 1 if kind == "queries" else 3
    masks = (step, step * SIDE, step * SIDE + step)
    return [
        lax.ppermute(v, "member", [(m, m ^ mask) for m in range(SIDE * SIDE)])
        for v, mask in zip(value, masks)
    ]


def scatter(at, place, ins, after=()):
    rows, cols = ins[0].shape
    piece = (rows // SIDE, cols)
    return call(
        functools.partial(scatter_kernel, place, len(ins)),
        [out(piece, F32)] + [out(piece, BF)] * (SIDE - 1),
        at,
        *ins,
        smem=(0,),
        scratch=[pltpu.VMEM((rows, cols), F32)],
        after=after,
        name="scatter",
    )


def exchanged(parts, axis):
    return [parts[0]] + [shift_by(parts[s], axis, s) for s in range(1, SIDE)]


def reduced(at, parts, after_z, after_x):
    parts = scatter(at, 1, parts, after_z)
    (piece,) = call(last_kernel, [out(parts[0].shape, BF)], *exchanged(parts, "y"), name="last")
    (piece,) = call(
        total_kernel, [out(piece.shape, BF)], *spread(piece, "x"), after=after_x, name="total"
    )
    return piece


def gathered(at, piece, after):
    rows, cols = piece.shape
    width = rows * 2 * SIDE * SIDE
    piece = jnp.concatenate(spread(piece[None], "y"), axis=0)
    (piece,) = call(
        stack_kernel,
        [out((SIDE * SIDE, rows, cols), BF)],
        *spread(piece, "z"),
        after=after,
        name="stack",
    )
    return call(
        place_kernel,
        [out((width, cols - width), F32), out((width, width), F32)],
        at,
        piece,
        shift_by(piece, "core", 1),
        smem=(0,),
        name="place",
    )


def local(hist_row, hist_owner, seq_len, item_table, neg_rows, in_weight, out_weight):
    devices = lax.axis_size(AXES)
    seqlen = hist_row.shape[1]
    owned, width = item_table.shape
    count = neg_rows.shape[1]
    group, member = lax.axis_index("group"), lax.axis_index("member")
    at = jnp.stack([member % SIDE, member // SIDE, group // 2, group % 2]).astype(jnp.int32)

    own_rows, own_bf = call(
        own_kernel,
        [out((count, width), BF), out((count, width), BF)],
        neg_rows,
        item_table,
        flops=2 * count * owned * width,
        name="own_negatives",
    )
    negs = [own_bf] + across([own_bf] * 3, "negatives")
    slots, requests = call(
        slots_kernel,
        [out((seqlen, 1), jnp.int32), out((devices, SLOTS), jnp.int32)],
        hist_owner.reshape(1, seqlen),
        hist_row,
        after=(own_bf,),
        name="slots",
    )
    asked = lax.all_to_all(requests, AXES, split_axis=0, concat_axis=0, tiled=True)
    (found,) = call(
        find_kernel,
        [out((devices * SLOTS, width), BF)],
        asked,
        item_table,
        flops=2 * devices * SLOTS * owned * width,
        after=(negs[1], negs[2]),
        name="find_rows",
    )
    back = lax.all_to_all(
        found.reshape(devices, SLOTS, width), AXES, split_axis=0, concat_axis=0, tiled=True
    ).reshape(devices * SLOTS, width)
    history, query, pos = call(
        forward_kernel,
        [out((seqlen, width), BF), out((seqlen, width), BF), out((8, seqlen), F32)],
        seq_len,
        back,
        slots,
        in_weight,
        out_weight,
        smem=(0,),
        scratch=[pltpu.VMEM((seqlen, width), F32)],
        flops=2 * seqlen * width * (devices * SLOTS + 6 * width),
        name="forward",
    )
    queries = [query] + across([query] * 3, "queries")
    weights, sums, totals = [], [], []
    for s, q in enumerate(queries):
        others = (*totals, pos) if s == SIDE - 1 else ()
        w, total, pack = call(
            functools.partial(scores_kernel, len(others)),
            [
                out((seqlen, SIDE * count), BF),
                out((seqlen, width), F32 if s == 0 else BF),
                out((8, seqlen), F32),
            ],
            q,
            *negs,
            *others,
            flops=4 * seqlen * SIDE * count * width,
            after=sums[:1],
            name="scores",
        )
        weights.append(w)
        sums.append(total)
        totals.append(pack)
    sums[1:] = across(sums[1:], "queries")
    packs = [pack] + across([pack] * 3, "queries")
    pre, mixed, output = call(
        again_kernel,
        [out((seqlen, 4 * width), F32), out((seqlen, width), F32), out((seqlen, width), F32)],
        seq_len,
        history,
        in_weight,
        out_weight,
        smem=(0,),
        flops=2 * seqlen * width * 6 * width,
        after=(pack,),
        name="layer_again",
    )
    *neg_parts, loss, factor = call(
        neg_kernel,
        [out((count, width), F32)]
        + [out((count, width), BF)] * (SIDE - 1)
        + [out((1, 1), F32), out((seqlen, 1), F32)],
        seq_len,
        *packs,
        *queries,
        *weights,
        smem=(0,),
        flops=2 * SIDE * seqlen * SIDE * count * width,
        after=(output,),
        name="negative_sums",
    )
    sent = across(neg_parts[1:], "negatives")
    row_grad, keep, send = call(
        backward_kernel,
        [
            out((seqlen, width), BF),
            out((width // 2, 5 * width), BF),
            out((width // 2, 5 * width), BF),
        ],
        seq_len,
        at,
        factor,
        *sums,
        history,
        pre,
        mixed,
        output,
        in_weight,
        out_weight,
        smem=(0, 1),
        scratch=[
            pltpu.VMEM((seqlen, width), BF),
            pltpu.VMEM((seqlen, width), BF),
            pltpu.VMEM((seqlen, 4 * width), BF),
        ],
        flops=2 * seqlen * width * 14 * width,
        name="backward",
    )
    got = shift_by(send, "core", 1)
    z_parts = exchanged(scatter(at, 2, [keep, got]), "z")
    (going,) = call(
        going_kernel,
        [out((devices * SLOTS, width), BF)],
        slots,
        row_grad,
        flops=2 * devices * SLOTS * seqlen * width,
        name="going",
    )
    arrived = lax.all_to_all(
        going.reshape(devices, SLOTS, width), AXES, split_axis=0, concat_axis=0, tiled=True
    ).reshape(devices * SLOTS, width)
    piece = reduced(at, z_parts, (*sent,), (arrived,))
    table_grad = table_grad_of(
        asked.reshape(1, devices * SLOTS), arrived, neg_rows, own_rows, [neg_parts[0], *sent], owned
    )
    in_grad, out_grad = gathered(at, piece, (table_grad,))
    return (loss.reshape(1), in_grad, out_grad, table_grad)


def solution(mesh):
    return jax.shard_map(
        local,
        mesh=mesh,
        in_specs=(
            P(AXES, None),
            P(AXES, None, None),
            P(AXES),
            P(AXES, None),
            P("group", "member"),
            P(),
            P(),
        ),
        out_specs=(P(AXES), P(), P(), P(AXES, None)),
        check_vma=False,
    )
```

time: 379 us -> 207 us (0.55)
  waiting for transfers between devices: 200 us -> 61 us
  starting transfers between devices: 13.5 us -> 64.8 us
  Pallas kernels: 0 us -> 46.2 us
  matrix products: 44.5 us -> 0 us
  other arithmetic: 38 us -> 0.92 us
  local copies, waits for them, and re-layouts: 43.5 us -> 15.3 us
  between operations: 16.7 us -> 1.98 us
  blocking collectives: 21.1 us -> 15.8 us
    psum x1 -> x0, waiting for transfers between devices: 153 us -> none  [local(): in_grad, out_grad = lax.psum((in_part, out_part), ('group', 'member'))]
    ppermute x0 -> x32, starting transfers between devices: none -> 49.9 us  [the longest x17 25.7 us: shift_by(): return lax.ppermute(value, name, pairs)]
    ppermute x0 -> x32, waiting for transfers between devices: none -> 47.5 us  [the longest x15 28.3 us: across(): lax.ppermute(v, 'member', [(m, m ^ mask) for m in range(SIDE * SIDE)])]
    pallas_call x0 -> x19, Pallas kernels: none -> 46.2 us  [the longest x18 40.8 us: call(): pl.pallas_call(body, out_shape=outs, in_specs=in_specs, out_specs=[pl.Blo...]
    dot_general x16 -> x0, matrix products: 44.5 us -> none  [the longest x3 10.5 us: hstu_layer(): jnp.dot(normed, in_wide.astype(jnp.bfloat16), preferred_element_type=jnp....]
    all_to_all x2, waiting for transfers between devices: 42.6 us -> 13.5 us  [the longest x1 13.5 us: local(): lax.all_to_all(found.reshape(devices, SLOTS, width), AXES, split_axis=0,...]
    scatter-add x2 -> x0, other arithmetic: 18 us -> none  [the longest x1 9.51 us: local(): table_grad.at[asked_rows.reshape(-1)].add(arrived.reshape(-1, model_width))]
    reshape x10 -> x1, local copies, waits for them, and re-layouts: 14.5 us -> 0.1 us  [local(): asked.reshape(1, devices * SLOTS)]
  transfers between devices with their start and end apart: 5 -> 34, of which waited for: 4 -> 15; matrix products, arithmetic and copies ran while one was open for 26% -> 1% of each run, Pallas kernels for 0% -> 14%
where the time goes in v1:
time: 207 us; the launch traced here: 206 us
  starting transfers between devices  64.8 us (31%)
  waiting for transfers between devices  61 us (29%)
  Pallas kernels  46.2 us (22%)
  blocking collectives  15.8 us (8%)
  local copies, waits for them, and re-layouts  15.3 us (7%)
    pallas_call x18, Pallas kernels, call(): pl.pallas_call(body, out_shape=outs, in_specs=in_specs, out_specs=[pl.Blo...  40.8 us
    ppermute x15, waiting for transfers between devices, across(): lax.ppermute(v, 'member', [(m, m ^ mask) for m in range(SIDE * SIDE)])  28.3 us
    ppermute x17, starting transfers between devices, shift_by(): return lax.ppermute(value, name, pairs)  25.7 us
    ppermute x15, starting transfers between devices, across(): lax.ppermute(v, 'member', [(m, m ^ mask) for m in range(SIDE * SIDE)])  24.2 us
    ppermute x17, waiting for transfers between devices, shift_by(): return lax.ppermute(value, name, pairs)  19.2 us
    all_to_all x1, blocking collectives, local(): lax.all_to_all(requests, AXES, split_axis=0, concat_axis=0, tiled=True)  15.8 us
    unnamed x68, local copies, waits for them, and re-layouts  14.7 us
    all_to_all x1, waiting for transfers between devices, local(): lax.all_to_all(found.reshape(devices, SLOTS, width), AXES, split_axis=0,...  13.5 us
  transfers between devices with their start and end apart: 34, of which 15 were waited for; matrix products, arithmetic and copies ran while one was open for 1% of the time, Pallas kernels for 14%

profile of v1, /device:TPU:1, one launch (start us, length us, event | category | flops | bytes accessed | tf_op | source)
XLA Modules:
  0.0 206.0 jit_solution(16140936693013925285)
XLA Ops:
  5.3 3.6 %collective-permute-start.1 = (bf16[512,512]{1,0:T(8,128)(2,1)S(1)}, bf16[512,512]{1,0:T(8,128)(2,1)S(1)}, u32[]{:S(2)}, u32[]{:S(2)}) collective-permute-start(bf16[512,512]{1,0:T(8,128)(2,1)S(1)} %get-tuple-element.45.refs_2_.refs_1_), channel_id=1, source_target_pairs={{0,12},{1,13},{2,14},{3,15},{4,8},{5,9},{6,10},{7,11},{8,4},{9,5},... | collective-permute-start | bytes 1572872 | tf_op jit(solution)/shard_map/ppermute | solution.py:522
  12.2 15.8 %all_to_all.21 = s32[128,1,8]{2,1,0:T(1,128)S(1)} all-to-all(s32[128,1,8]{2,1,0:T(1,128)S(1)} %bitcast.24), channel_id=1, replica_groups=mesh['group'=8,'member'=16] {'group','member'}, dimensions={0} | all-to-all | bytes 8192 | tf_op jit(solution)/shard_map/all_to_all | solution.py:602
  28.1 3.2 %find_rows.1 = bf16[1024,512]{1,0:T(8,128)(2,1)S(1)} custom-call(s32[128,8]{1,0:T(8,128)S(1)} %bitcast.23, bf16[2048,512]{1,0:T(8,128)(2,1)S(1)} %copy-done.21, bf16[512,512]{1,0:T(8,128)(2,1)S(1)} %collective-permute-done.refs_2_, bf16[512,512]{1,0:T(8,128)(2,1)S(1)} %collective-permute-done.1.refs_3_), custom_call_target="tpu_custom_call" | custom-call | flops 2147483648 | bytes 3149824 | tf_op jit(solution)/shard_map/find_rows/pallas_call | solution.py:140
  32.2 7.4 %all-to-all-start.1 = ((bf16[128,8,512]{2,1,0:T(8,128)(2,1)}), bf16[128,8,512]{2,1,0:T(8,128)(2,1)S(1)}, u32[]{:S(2)}, u32[]{:S(2)}) async-start(bf16[128,8,512]{2,1,0:T(8,128)(2,1)} %bitcast.18), calls=%async_computation.1 | async-start | bytes 2097152 | tf_op jit(solution)/shard_map/all_to_all | solution.py:612
  39.6 4.9 %collective-permute-start.3 = (bf16[512,512]{1,0:T(8,128)(2,1)}, bf16[512,512]{1,0:T(8,128)(2,1)}, u32[]{:S(2)}, u32[]{:S(2)}) collective-permute-start(bf16[512,512]{1,0:T(8,128)(2,1)} %copy-done.5), channel_id=1, source_target_pairs={{0,15},{1,14},{2,13},{3,12},{4,11},{5,10},{6,9},{7,8},{8,7},{9,6},... | collective-permute-start | bytes 1572872 | tf_op jit(solution)/shard_map/ppermute | solution.py:522
  45.1 13.5 %all-to-all-done.1 = bf16[128,8,512]{2,1,0:T(8,128)(2,1)S(1)} async-done(((bf16[128,8,512]{2,1,0:T(8,128)(2,1)}), bf16[128,8,512]{2,1,0:T(8,128)(2,1)S(1)}, u32[]{:S(2)}, u32[]{:S(2)}) %all-to-all-start.1) | async-done | bytes 1048608 | tf_op jit(solution)/shard_map/all_to_all | solution.py:612
  60.6 3.2 %forward.1 = (bf16[256,512]{1,0:T(8,128)(2,1)S(1)}, bf16[256,512]{1,0:T(8,128)(2,1)}, f32[8,256]{1,0:T(8,128)S(1)}) custom-call(s32[1]{0:T(128)S(6)} %copy.12.refs_0_, bf16[1024,512]{1,0:T(8,128)(2,1)S(1)} %bitcast.17, s32[256,1]{1,0:T(8,128)S(1)} %copy-done.17, bf16[512,2048]{1,0:T(8,128)(2,1)S(1)} %copy-done.1, bf16[512,512]{1,0:T(8,128)(2,1)S(1)} %copy-done.3), custom_call_target="tpu_custom_call" | custom-call | flops 1073741824 | bytes 4203524 | tf_op jit(solution)/shard_map/forward/pallas_call | solution.py:140
  70.2 2.7 %scores.4 = (bf16[256,2048]{1,0:T(8,128)(2,1)S(1)}, f32[256,512]{1,0:T(8,128)S(1)}, f32[8,256]{1,0:T(8,128)S(1)}) custom-call(bf16[256,512]{1,0:T(8,128)(2,1)} %get-tuple-element.48.refs_0_.refs_5_, bf16[512,512]{1,0:T(8,128)(2,1)S(1)} %copy-done.6, bf16[512,512]{1,0:T(8,128)(2,1)S(1)} %copy-done.26, bf16[512,512]{1,0:T(8,128)(2,1)S(1)} %copy-done.23, ...), custom_call_target="tpu_custom_call" | custom-call | flops 1073741824 | bytes 3940352 | tf_op jit(solution)/shard_map/scores/pallas_call | solution.py:140
  75.7 2.7 %scores.5 = (bf16[256,2048]{1,0:T(8,128)(2,1)S(1)}, bf16[256,512]{1,0:T(8,128)(2,1)S(1)}, f32[8,256]{1,0:T(8,128)S(1)}) custom-call(bf16[256,512]{1,0:T(8,128)(2,1)S(1)} %collective-permute-done.4.refs_0_.refs_6_, bf16[512,512]{1,0:T(8,128)(2,1)S(1)} %copy-done.6, bf16[512,512]{1,0:T(8,128)(2,1)S(1)} %copy-done.26, bf16[512,512]{1,0:T(8,128)(2,1)S(1)} %copy-done.23, ...), custom_call_target="tpu_custom_call" | custom-call | flops 1073741824 | bytes 3678208 | tf_op jit(solution)/shard_map/scores/pallas_call | solution.py:140
  78.5 2.7 %scores.7 = (bf16[256,2048]{1,0:T(8,128)(2,1)S(1)}, bf16[256,512]{1,0:T(8,128)(2,1)S(1)}, f32[8,256]{1,0:T(8,128)S(1)}) custom-call(bf16[256,512]{1,0:T(8,128)(2,1)S(1)} %collective-permute-done.2.refs_0_.refs_8_, bf16[512,512]{1,0:T(8,128)(2,1)S(1)} %copy-done.7, bf16[512,512]{1,0:T(8,128)(2,1)S(1)} %copy-done.27, bf16[512,512]{1,0:T(8,128)(2,1)S(1)} %copy-done.24, ...), custom_call_target="tpu_custom_call" | custom-call | flops 1073741824 | bytes 3710976 | tf_op jit(solution)/shard_map/scores/pallas_call | solution.py:140
  88.7 4.5 %negative_sums.1 = (f32[512,512]{1,0:T(8,128)S(1)}, bf16[512,512]{1,0:T(8,128)(2,1)}, bf16[512,512]{1,0:T(8,128)(2,1)}, bf16[512,512]{1,0:T(8,128)(2,1)}, f32[1,1]{1,0:T(1,128)}, /*index=5*/f32[256,1]{1,0:T(8,128)S(1)}) custom-call(s32[1]{0:T(128)S(6)} %copy.12.refs_0_, f32[8,256]{1,0:T(8,128)S(1)} %get-tuple-element.54.refs_4_.refs_1_, ...), custom_call_target="tpu_custom_call" | custom-call | flops 2147483648 | bytes 7898120 | tf_op jit(solution)/shard_map/negative_sums/pallas_call | solution.py:140
  93.3 3.8 %collective-permute-done.10.refs_5_ = bf16[256,512]{1,0:T(8,128)(2,1)S(1)} collective-permute-done((bf16[256,512]{1,0:T(8,128)(2,1)S(1)}, bf16[256,512]{1,0:T(8,128)(2,1)S(1)}, u32[]{:S(2)}, u32[]{:S(2)}) %collective-permute-start.10) | collective-permute-done | bytes 262176 | tf_op jit(solution)/shard_map/ppermute | solution.py:522
  97.1 5.9 %backward.1 = (bf16[256,512]{1,0:T(8,128)(2,1)S(1)}, bf16[256,2560]{1,0:T(8,128)(2,1)S(1)}, bf16[256,2560]{1,0:T(8,128)(2,1)}) custom-call(s32[1]{0:T(128)S(6)} %copy.12.refs_0_, s32[4]{0:T(128)S(1)} %pad_add_fusion.refs_1_.refs_0_, f32[256,1]{1,0:T(8,128)S(1)} %get-tuple-element.62.refs_2_, f32[256,512]{1,0:T(8,128)S(1)} %get-tuple-element.50.refs_5_.refs_9_.refs_3_, ...), custom_call_target="tpu_custom_call" | custom-call | flops 1879048192 | bytes 10224660 | tf_op jit(solution)/shard_map/backward/pallas_call | solution.py:140
  107.2 7.5 %all-to-all-start.2 = ((bf16[128,8,512]{2,1,0:T(8,128)(2,1)}), bf16[128,8,512]{2,1,0:T(8,128)(2,1)S(1)}, u32[]{:S(2)}, u32[]{:S(2)}) async-start(bf16[128,8,512]{2,1,0:T(8,128)(2,1)} %bitcast.11), calls=%async_computation.2 | async-start | bytes 2097152 | tf_op jit(solution)/shard_map/all_to_all | solution.py:714
  123.3 2.9 %collective-permute-start.14 = (bf16[64,2560]{1,0:T(8,128)(2,1)S(1)}, bf16[64,2560]{1,0:T(8,128)(2,1)S(1)}, u32[]{:S(2)}, u32[]{:S(2)}) collective-permute-start(bf16[64,2560]{1,0:T(8,128)(2,1)S(1)} %get-tuple-element.72), channel_id=1, source_target_pairs={{0,64},{16,80},{32,96},{48,112},{64,0},{80,16},{96,32},{112,48},{1... | collective-permute-start | bytes 983048 | tf_op jit(solution)/shard_map/ppermute | solution.py:511
  126.3 13.6 %collective-permute-done.16.refs_5_.neg1 = bf16[512,512]{1,0:T(8,128)(2,1)S(1)} collective-permute-done((bf16[512,512]{1,0:T(8,128)(2,1)}, bf16[512,512]{1,0:T(8,128)(2,1)S(1)}, u32[]{:S(2)}, u32[]{:S(2)}) %collective-permute-start.16) | collective-permute-done | bytes 524320 | tf_op jit(solution)/shard_map/ppermute | solution.py:522
  139.9 3.1 %collective-permute-start.15 = (bf16[64,2560]{1,0:T(8,128)(2,1)S(1)}, bf16[64,2560]{1,0:T(8,128)(2,1)S(1)}, u32[]{:S(2)}, u32[]{:S(2)}) collective-permute-start(bf16[64,2560]{1,0:T(8,128)(2,1)S(1)} %get-tuple-element.73), channel_id=1, source_target_pairs={{0,96},{16,112},{32,0},{48,16},{64,32},{80,48},{96,64},{112,80},{1... | collective-permute-start | bytes 983048 | tf_op jit(solution)/shard_map/ppermute | solution.py:511
  143.0 10.3 %collective-permute-done.18.refs_7_.neg3 = bf16[512,512]{1,0:T(8,128)(2,1)S(1)} collective-permute-done((bf16[512,512]{1,0:T(8,128)(2,1)}, bf16[512,512]{1,0:T(8,128)(2,1)S(1)}, u32[]{:S(2)}, u32[]{:S(2)}) %collective-permute-start.18) | collective-permute-done | bytes 524320 | tf_op jit(solution)/shard_map/ppermute | solution.py:522
  156.9 2.8 %collective-permute-done.19.refs_1_ = bf16[16,2560]{1,0:T(8,128)(2,1)S(1)} collective-permute-done((bf16[16,2560]{1,0:T(8,128)(2,1)S(1)}, bf16[16,2560]{1,0:T(8,128)(2,1)S(1)}, u32[]{:S(2)}, u32[]{:S(2)}) %collective-permute-start.19) | collective-permute-done | bytes 81952 | tf_op jit(solution)/shard_map/ppermute | solution.py:511
  174.6 3.3 %collective-permute-start.30 = (bf16[4,16,2560]{2,1,0:T(8,128)(2,1)S(1)}, bf16[4,16,2560]{2,1,0:T(8,128)(2,1)S(1)}, u32[]{:S(2)}, u32[]{:S(2)}) collective-permute-start(bf16[4,16,2560]{2,1,0:T(8,128)(2,1)S(1)} %pad_maximum_fusion.refs_0_), channel_id=1, source_target_pairs={{0,96},{16,112},{32,0},{48,16},{64,32},{80,48},{96,64},{112,80},{1... | collective-permute-start | bytes 983048 | tf_op jit(solution)/shard_map/ppermute | solution.py:511
  183.5 5.4 %table_grad.1.refs_4_ = f32[2048,512]{1,0:T(8,128)} custom-call(s32[1,1024]{1,0:T(1,128)S(1)} %reshape.38.asked_ref, bf16[1024,512]{1,0:T(8,128)(2,1)S(1)} %bitcast.16, s32[1,512]{1,0:T(1,128)S(1)} %copy-done.29, bf16[512,512]{1,0:T(8,128)(2,1)S(1)} %copy-done.33, f32[512,512]{1,0:T(8,128)S(1)} %copy-done.31, bf16[512,512]{1,0:T(8,128)(2,1)S(1)} %copy-done.9, ...), custom_call_target="tpu_custom_call" | custom-call | flops 3221225472 | bytes 4194304 | tf_op jit(solution)/shard_map/table_grad/pallas_call | solution.py:429
  188.9 4.0 %collective-permute-done.28.refs_1_ = bf16[4,16,2560]{2,1,0:T(8,128)(2,1)} collective-permute-done((bf16[4,16,2560]{2,1,0:T(8,128)(2,1)S(1)}, bf16[4,16,2560]{2,1,0:T(8,128)(2,1)}, u32[]{:S(2)}, u32[]{:S(2)}) %collective-permute-start.28) | collective-permute-done | bytes 327712 | tf_op jit(solution)/shard_map/ppermute | solution.py:511
  196.3 3.6 %collective-permute-start.31 = (bf16[16,16,2560]{2,1,0:T(8,128)(2,1)S(1)}, bf16[16,16,2560]{2,1,0:T(8,128)(2,1)S(1)}, u32[]{:S(2)}, u32[]{:S(2)}) collective-permute-start(bf16[16,16,2560]{2,1,0:T(8,128)(2,1)S(1)} %stack.21.refs_1_), channel_id=1, source_target_pairs={{0,16},{16,0},{32,48},{48,32},{64,80},{80,64},{96,112},{112,96},{1... | collective-permute-start | bytes 3932168 | tf_op jit(solution)/shard_map/ppermute | solution.py:511
  202.5 3.2 %place.1 = (f32[512,2048]{1,0:T(8,128)}, f32[512,512]{1,0:T(8,128)}) custom-call(s32[4]{0:T(128)S(1)} %pad_add_fusion.refs_1_.refs_0_, bf16[16,16,2560]{2,1,0:T(8,128)(2,1)S(1)} %stack.21.refs_1_, bf16[16,16,2560]{2,1,0:T(8,128)(2,1)S(1)} %collective-permute-done.31.refs_2_), custom_call_target="tpu_custom_call" | custom-call | bytes 7864336 | tf_op jit(solution)/shard_map/place/pallas_call | solution.py:140
  (137 shorter events, 70.2 us)
Async XLA Ops:
  5.3 22.7 %collective-permute-start.1 = (bf16[512,512]{1,0:T(8,128)(2,1)S(1)}, bf16[512,512]{1,0:T(8,128)(2,1)S(1)}, u32[]{:S(2)}, u32[]{:S(2)}) collective-permute-start(bf16[512,512]{1,0:T(8,128)(2,1)S(1)} %get-tuple-element.45.refs_2_.refs_1_), channel_id=1, source_target_pairs={{0,12},{1,13},{2,14},{3,15},{4,8},{5,9},{6,10},{7,11},{8,4},{9,5},... | collective-permute-start | bytes 1572872 | tf_op jit(solution)/shard_map/ppermute | solution.py:522
  8.9 19.1 %collective-permute-start = (bf16[512,512]{1,0:T(8,128)(2,1)S(1)}, bf16[512,512]{1,0:T(8,128)(2,1)S(1)}, u32[]{:S(2)}, u32[]{:S(2)}) collective-permute-start(bf16[512,512]{1,0:T(8,128)(2,1)S(1)} %get-tuple-element.45.refs_2_.refs_1_), channel_id=1, source_target_pairs={{0,3},{1,2},{2,1},{3,0},{4,7},{5,6},{6,5},{7,4},{8,11},{9,10},{10,... | collective-permute-start | bytes 1572872 | tf_op jit(solution)/shard_map/ppermute | solution.py:522
  32.2 26.4 %all-to-all-start.1 = ((bf16[128,8,512]{2,1,0:T(8,128)(2,1)}), bf16[128,8,512]{2,1,0:T(8,128)(2,1)S(1)}, u32[]{:S(2)}, u32[]{:S(2)}) async-start(bf16[128,8,512]{2,1,0:T(8,128)(2,1)} %bitcast.18), calls=%async_computation.1 | async-start | bytes 2097152 | tf_op jit(solution)/shard_map/all_to_all | solution.py:612
  39.6 27.5 %collective-permute-start.3 = (bf16[512,512]{1,0:T(8,128)(2,1)}, bf16[512,512]{1,0:T(8,128)(2,1)}, u32[]{:S(2)}, u32[]{:S(2)}) collective-permute-start(bf16[512,512]{1,0:T(8,128)(2,1)} %copy-done.5), channel_id=1, source_target_pairs={{0,15},{1,14},{2,13},{3,12},{4,11},{5,10},{6,9},{7,8},{8,7},{9,6},... | collective-permute-start | bytes 1572872 | tf_op jit(solution)/shard_map/ppermute | solution.py:522
  63.8 9.2 %collective-permute-start.5 = (bf16[256,512]{1,0:T(8,128)(2,1)}, bf16[256,512]{1,0:T(8,128)(2,1)S(1)}, u32[]{:S(2)}, u32[]{:S(2)}) collective-permute-start(bf16[256,512]{1,0:T(8,128)(2,1)} %get-tuple-element.48.refs_0_.refs_5_), channel_id=1, source_target_pairs={{0,4},{1,5},{2,6},{3,7},{4,0},{5,1},{6,2},{7,3},{8,12},{9,13},{10,... | collective-permute-start | bytes 786440 | tf_op jit(solution)/shard_map/ppermute | solution.py:522
  64.6 11.1 %collective-permute-start.4 = (bf16[256,512]{1,0:T(8,128)(2,1)}, bf16[256,512]{1,0:T(8,128)(2,1)S(1)}, u32[]{:S(2)}, u32[]{:S(2)}) collective-permute-start(bf16[256,512]{1,0:T(8,128)(2,1)} %get-tuple-element.48.refs_0_.refs_5_), channel_id=1, source_target_pairs={{0,1},{1,0},{2,3},{3,2},{4,5},{5,4},{6,7},{7,6},{8,9},{9,8},{10,11... | collective-permute-start | bytes 786440 | tf_op jit(solution)/shard_map/ppermute | solution.py:522
  64.9 13.5 %collective-permute-start.2 = (bf16[256,512]{1,0:T(8,128)(2,1)}, bf16[256,512]{1,0:T(8,128)(2,1)S(1)}, u32[]{:S(2)}, u32[]{:S(2)}) collective-permute-start(bf16[256,512]{1,0:T(8,128)(2,1)} %get-tuple-element.48.refs_0_.refs_5_), channel_id=1, source_target_pairs={{0,5},{1,4},{2,7},{3,6},{4,1},{5,0},{6,3},{7,2},{8,13},{9,12},{10,... | collective-permute-start | bytes 786440 | tf_op jit(solution)/shard_map/ppermute | solution.py:522
  81.5 7.2 %collective-permute-start.7 = (f32[8,256]{1,0:T(8,128)S(1)}, f32[8,256]{1,0:T(8,128)S(1)}, u32[]{:S(2)}, u32[]{:S(2)}) collective-permute-start(f32[8,256]{1,0:T(8,128)S(1)} %get-tuple-element.54.refs_4_.refs_1_), channel_id=1, source_target_pairs={{0,4},{1,5},{2,6},{3,7},{4,0},{5,1},{6,2},{7,3},{8,12},{9,13},{10,... | collective-permute-start | bytes 24584 | tf_op jit(solution)/shard_map/ppermute | solution.py:522
  82.7 6.0 %collective-permute-start.6 = (f32[8,256]{1,0:T(8,128)S(1)}, f32[8,256]{1,0:T(8,128)S(1)}, u32[]{:S(2)}, u32[]{:S(2)}) collective-permute-start(f32[8,256]{1,0:T(8,128)S(1)} %get-tuple-element.54.refs_4_.refs_1_), channel_id=1, source_target_pairs={{0,1},{1,0},{2,3},{3,2},{4,5},{5,4},{6,7},{7,6},{8,9},{9,8},{10,11... | collective-permute-start | bytes 24584 | tf_op jit(solution)/shard_map/ppermute | solution.py:522
  84.0 13.1 %collective-permute-start.10 = (bf16[256,512]{1,0:T(8,128)(2,1)S(1)}, bf16[256,512]{1,0:T(8,128)(2,1)S(1)}, u32[]{:S(2)}, u32[]{:S(2)}) collective-permute-start(bf16[256,512]{1,0:T(8,128)(2,1)S(1)} %get-tuple-element.64), channel_id=1, source_target_pairs={{0,4},{1,5},{2,6},{3,7},{4,0},{5,1},{6,2},{7,3},{8,12},{9,13},{10,... | collective-permute-start | bytes 786440 | tf_op jit(solution)/shard_map/ppermute | solution.py:522
  84.1 12.9 %collective-permute-start.11 = (bf16[256,512]{1,0:T(8,128)(2,1)S(1)}, bf16[256,512]{1,0:T(8,128)(2,1)S(1)}, u32[]{:S(2)}, u32[]{:S(2)}) collective-permute-start(bf16[256,512]{1,0:T(8,128)(2,1)S(1)} %get-tuple-element.65), channel_id=1, source_target_pairs={{0,5},{1,4},{2,7},{3,6},{4,1},{5,0},{6,3},{7,2},{8,13},{9,12},{10,... | collective-permute-start | bytes 786440 | tf_op jit(solution)/shard_map/ppermute | solution.py:522
  85.4 11.7 %collective-permute-start.9 = (bf16[256,512]{1,0:T(8,128)(2,1)S(1)}, bf16[256,512]{1,0:T(8,128)(2,1)S(1)}, u32[]{:S(2)}, u32[]{:S(2)}) collective-permute-start(bf16[256,512]{1,0:T(8,128)(2,1)S(1)} %get-tuple-element.63), channel_id=1, source_target_pairs={{0,1},{1,0},{2,3},{3,2},{4,5},{5,4},{6,7},{7,6},{8,9},{9,8},{10,11... | collective-permute-start | bytes 786440 | tf_op jit(solution)/shard_map/ppermute | solution.py:522
  103.0 16.9 %collective-permute-start.12 = (bf16[256,2560]{1,0:T(8,128)(2,1)}, bf16[256,2560]{1,0:T(8,128)(2,1)}, u32[]{:S(2)}, u32[]{:S(2)}) collective-permute-start(bf16[256,2560]{1,0:T(8,128)(2,1)} %get-tuple-element.69), channel_id=1, source_target_pairs={{0,16},{16,0},{32,48},{48,32},{64,80},{80,64},{96,112},{112,96},{1... | collective-permute-start | bytes 3932168 | tf_op jit(solution)/shard_map/ppermute | solution.py:511
  107.2 55.5 %all-to-all-start.2 = ((bf16[128,8,512]{2,1,0:T(8,128)(2,1)}), bf16[128,8,512]{2,1,0:T(8,128)(2,1)S(1)}, u32[]{:S(2)}, u32[]{:S(2)}) async-start(bf16[128,8,512]{2,1,0:T(8,128)(2,1)} %bitcast.11), calls=%async_computation.2 | async-start | bytes 2097152 | tf_op jit(solution)/shard_map/all_to_all | solution.py:714
  114.7 25.2 %collective-permute-start.16 = (bf16[512,512]{1,0:T(8,128)(2,1)}, bf16[512,512]{1,0:T(8,128)(2,1)S(1)}, u32[]{:S(2)}, u32[]{:S(2)}) collective-permute-start(bf16[512,512]{1,0:T(8,128)(2,1)} %get-tuple-element.74), channel_id=1, source_target_pairs={{0,3},{1,2},{2,1},{3,0},{4,7},{5,6},{6,5},{7,4},{8,11},{9,10},{10,... | collective-permute-start | bytes 1572872 | tf_op jit(solution)/shard_map/ppermute | solution.py:522
  117.4 25.6 %collective-permute-start.17 = (bf16[512,512]{1,0:T(8,128)(2,1)}, bf16[512,512]{1,0:T(8,128)(2,1)S(1)}, u32[]{:S(2)}, u32[]{:S(2)}) collective-permute-start(bf16[512,512]{1,0:T(8,128)(2,1)} %get-tuple-element.75), channel_id=1, source_target_pairs={{0,12},{1,13},{2,14},{3,15},{4,8},{5,9},{6,10},{7,11},{8,4},{9,5},... | collective-permute-start | bytes 1572872 | tf_op jit(solution)/shard_map/ppermute | solution.py:522
  119.9 33.5 %collective-permute-start.18 = (bf16[512,512]{1,0:T(8,128)(2,1)}, bf16[512,512]{1,0:T(8,128)(2,1)S(1)}, u32[]{:S(2)}, u32[]{:S(2)}) collective-permute-start(bf16[512,512]{1,0:T(8,128)(2,1)} %get-tuple-element.76), channel_id=1, source_target_pairs={{0,15},{1,14},{2,13},{3,12},{4,11},{5,10},{6,9},{7,8},{8,7},{9,6},... | collective-permute-start | bytes 1572872 | tf_op jit(solution)/shard_map/ppermute | solution.py:522
  121.8 31.5 %collective-permute-start.13 = (bf16[64,2560]{1,0:T(8,128)(2,1)S(1)}, bf16[64,2560]{1,0:T(8,128)(2,1)S(1)}, u32[]{:S(2)}, u32[]{:S(2)}) collective-permute-start(bf16[64,2560]{1,0:T(8,128)(2,1)S(1)} %get-tuple-element.71), channel_id=1, source_target_pairs={{0,32},{16,48},{32,64},{48,80},{64,96},{80,112},{96,0},{112,16},{1... | collective-permute-start | bytes 983048 | tf_op jit(solution)/shard_map/ppermute | solution.py:511
  123.3 30.0 %collective-permute-start.14 = (bf16[64,2560]{1,0:T(8,128)(2,1)S(1)}, bf16[64,2560]{1,0:T(8,128)(2,1)S(1)}, u32[]{:S(2)}, u32[]{:S(2)}) collective-permute-start(bf16[64,2560]{1,0:T(8,128)(2,1)S(1)} %get-tuple-element.72), channel_id=1, source_target_pairs={{0,64},{16,80},{32,96},{48,112},{64,0},{80,16},{96,32},{112,48},{1... | collective-permute-start | bytes 983048 | tf_op jit(solution)/shard_map/ppermute | solution.py:511
  139.9 13.5 %collective-permute-start.15 = (bf16[64,2560]{1,0:T(8,128)(2,1)S(1)}, bf16[64,2560]{1,0:T(8,128)(2,1)S(1)}, u32[]{:S(2)}, u32[]{:S(2)}) collective-permute-start(bf16[64,2560]{1,0:T(8,128)(2,1)S(1)} %get-tuple-element.73), channel_id=1, source_target_pairs={{0,96},{16,112},{32,0},{48,16},{64,32},{80,48},{96,64},{112,80},{1... | collective-permute-start | bytes 983048 | tf_op jit(solution)/shard_map/ppermute | solution.py:511
  174.6 14.4 %collective-permute-start.30 = (bf16[4,16,2560]{2,1,0:T(8,128)(2,1)S(1)}, bf16[4,16,2560]{2,1,0:T(8,128)(2,1)S(1)}, u32[]{:S(2)}, u32[]{:S(2)}) collective-permute-start(bf16[4,16,2560]{2,1,0:T(8,128)(2,1)S(1)} %pad_maximum_fusion.refs_0_), channel_id=1, source_target_pairs={{0,96},{16,112},{32,0},{48,16},{64,32},{80,48},{96,64},{112,80},{1... | collective-permute-start | bytes 983048 | tf_op jit(solution)/shard_map/ppermute | solution.py:511
  177.8 11.1 %collective-permute-start.29 = (bf16[4,16,2560]{2,1,0:T(8,128)(2,1)S(1)}, bf16[4,16,2560]{2,1,0:T(8,128)(2,1)}, u32[]{:S(2)}, u32[]{:S(2)}) collective-permute-start(bf16[4,16,2560]{2,1,0:T(8,128)(2,1)S(1)} %pad_maximum_fusion.refs_0_), channel_id=1, source_target_pairs={{0,64},{16,80},{32,96},{48,112},{64,0},{80,16},{96,32},{112,48},{1... | collective-permute-start | bytes 983048 | tf_op jit(solution)/shard_map/ppermute | solution.py:511
  178.0 15.0 %collective-permute-start.28 = (bf16[4,16,2560]{2,1,0:T(8,128)(2,1)S(1)}, bf16[4,16,2560]{2,1,0:T(8,128)(2,1)}, u32[]{:S(2)}, u32[]{:S(2)}) collective-permute-start(bf16[4,16,2560]{2,1,0:T(8,128)(2,1)S(1)} %pad_maximum_fusion.refs_0_), channel_id=1, source_target_pairs={{0,32},{16,48},{32,64},{48,80},{64,96},{80,112},{96,0},{112,16},{1... | collective-permute-start | bytes 983048 | tf_op jit(solution)/shard_map/ppermute | solution.py:511
  196.3 6.2 %collective-permute-start.31 = (bf16[16,16,2560]{2,1,0:T(8,128)(2,1)S(1)}, bf16[16,16,2560]{2,1,0:T(8,128)(2,1)S(1)}, u32[]{:S(2)}, u32[]{:S(2)}) collective-permute-start(bf16[16,16,2560]{2,1,0:T(8,128)(2,1)S(1)} %stack.21.refs_1_), channel_id=1, source_target_pairs={{0,16},{16,0},{32,48},{48,32},{64,80},{80,64},{96,112},{112,96},{1... | collective-permute-start | bytes 3932168 | tf_op jit(solution)/shard_map/ppermute | solution.py:511
  (44 other events, 332.1 us)

commit v2 on v1

--- a/solution.py
+++ b/solution.py
@@ -154,6 +154,20 @@
 
 def out(shape, dtype):
     return jax.ShapeDtypeStruct(shape, dtype)
+
+
+def later(values, after):
+    count = len(values)
+    anywhere = pl.BlockSpec(memory_space=pl.ANY)
+    return pl.pallas_call(
+        lambda *refs: None,
+        out_shape=[out(v.shape, v.dtype) for v in values],
+        in_specs=[anywhere] * (count + len(after)),
+        out_specs=[anywhere] * count,
+        input_output_aliases={i: i for i in range(count)},
+        cost_estimate=pl.CostEstimate(flops=0, bytes_accessed=0, transcendentals=0),
+        name="later",
+    )(*values, *after)
 
 
 def slots_kernel(owner_ref, row_ref, slots_ref, req_ref):
@@ -257,13 +271,14 @@
     pos_ref[...] = jnp.where(iota(rows.shape, 0) == 0, rows, usable)
 
 
-def again_kernel(len_ref, hist_ref, in_ref, out_ref, pre_ref, mixed_ref, output_ref):
+def again_kernel(
+    len_ref, hist_ref, in_ref, out_ref, pre_ref, mixed_ref, output_ref
+):
     output_ref[...] = layer(len_ref[0], hist_ref[...], in_ref, out_ref, mixed_ref, pre_ref)
 
 
-def scores_kernel(count, query_ref, *refs):
-    negs, others = refs[:SIDE], refs[SIDE : SIDE + count]
-    weights_ref, grad_ref, total_ref = refs[-3:]
+def scores_kernel(query_ref, *refs):
+    negs, others, (weights_ref, grad_ref, total_ref) = refs[:SIDE], refs[SIDE:-3], refs[-3:]
     query = query_ref[...]
     total = jnp.zeros((query.shape[0], 1), F32)
     grad = jnp.zeros(query.shape, F32)
@@ -292,7 +307,8 @@
 
 def neg_kernel(len_ref, *refs):
     packs, queries, weights = refs[:SIDE], refs[SIDE : 2 * SIDE], refs[2 * SIDE : 3 * SIDE]
-    outs, (loss_ref, factor_ref) = refs[3 * SIDE : -2], refs[-2:]
+    own_ref, first_ref, second_ref, third_ref, last_ref, loss_ref, factor_ref = refs[3 * SIDE :]
+    half = own_ref.shape[1] // 2
     scaled = []
     for k, query_ref in enumerate(queries):
         pos_score, usable = packs[k][SIDE : SIDE + 1, :], packs[k][SIDE + 1 : SIDE + 2, :]
@@ -307,13 +323,28 @@
         if k == 0:
             factor_ref[...] = factor
         scaled.append((query_ref[...].astype(F32) * factor).astype(BF))
-    for k, ref in enumerate(outs):
-        size = ref.shape[0]
+    for k in range(SIDE):
+        size = own_ref.shape[0]
         cols = slice(k * size, (k + 1) * size)
         total = mm_tn(weights[0][:, cols], scaled[0])
         for w, q in zip(weights[1:], scaled[1:]):
             total = total + mm_tn(w[:, cols], q)
-        ref[...] = total.astype(ref.dtype)
+        left, right = total[:, :half].astype(BF), total[:, half:].astype(BF)
+        if k == 0:
+            own_ref[...] = total
+        elif k == 1:
+            first_ref[0], last_ref[...] = left, right
+        elif k == 2:
+            third_ref[...], second_ref[0] = left, right
+        else:
+            first_ref[1], second_ref[1] = left, right
+
+
+def turn_kernel(third_ref, from_first, last_ref, from_second, over_third, over_last):
+    third = third_ref[...].astype(F32) + from_first[1].astype(F32)
+    over_third[...] = third.astype(BF)
+    last = last_ref[...].astype(F32) + from_second[1].astype(F32)
+    over_last[...] = last.astype(BF)
 
 
 def backward_kernel(
@@ -401,7 +432,8 @@
 
 
 def table_kernel(
-    asked_ref, arrived_ref, ids_ref, rows_ref, neg0, neg1, neg2, neg3, table_ref, grad_ref
+    asked_ref, arrived_ref, ids_ref, rows_ref, own_ref, first_ref, second_ref, third_ref, last_ref,
+    table_ref, done_ref, grad_ref,
 ):
     block = table_ref.shape[0]
 
@@ -410,9 +442,12 @@
         rows = rows_ref[...].astype(F32)
         scale = lax.rsqrt(jnp.sum(rows * rows, axis=-1, keepdims=True) + 1e-06)
         unit = rows * scale
-        total = neg0[...] + neg1[...].astype(F32) + neg2[...].astype(F32) + neg3[...].astype(F32)
+        left = first_ref[0].astype(F32) + third_ref[...].astype(F32)
+        right = second_ref[0].astype(F32) + last_ref[...].astype(F32)
+        total = own_ref[...] + jnp.concatenate([left, right], axis=1)
         grad = scale * (total - unit * jnp.sum(unit * total, axis=-1, keepdims=True))
         grad_ref[...] = grad.astype(BF)
+        done_ref[...] = jnp.zeros(done_ref.shape, F32)
 
     first = pl.program_id(0) * block
     asked, ids = asked_ref[...], ids_ref[...]
@@ -429,9 +464,12 @@
     return pl.pallas_call(
         table_kernel,
         grid=(owned // block,),
-        out_shape=out((owned, width), F32),
-        in_specs=[whole] * 8,
-        out_specs=pl.BlockSpec((block, width), lambda i: (i, 0)),
+        out_shape=[out((owned, width), F32), out((8, 128), F32)],
+        in_specs=[whole] * 9,
+        out_specs=[
+            pl.BlockSpec((block, width), lambda i: (i, 0)),
+            pl.BlockSpec((8, 128), lambda i: (0, 0)),
+        ],
         scratch_shapes=[pltpu.VMEM(rows.shape, BF)],
         compiler_params=pltpu.CompilerParams(vmem_limit_bytes=40 * MIB),
         cost_estimate=pl.CostEstimate(
@@ -515,12 +553,18 @@
     return [value] + [shift_by(value, axis, s) for s in range(1, SIDE)]
 
 
+def square(value, axis):
+    step = 3 if axis == "x" else 3 * SIDE
+    return lax.ppermute(value, "member", [(m, m ^ step) for m in range(SIDE * SIDE)])
+
+
 def across(value, kind):
     step = 1 if kind == "queries" else 3
     masks = (step, step * SIDE, step * SIDE + step)
     return [
         lax.ppermute(v, "member", [(m, m ^ mask) for m in range(SIDE * SIDE)])
         for v, mask in zip(value, masks)
+        if v is not None
     ]
 
 
@@ -543,11 +587,10 @@
     return [parts[0]] + [shift_by(parts[s], axis, s) for s in range(1, SIDE)]
 
 
-def reduced(at, parts, after_z, after_x):
-    parts = scatter(at, 1, parts, after_z)
+def reduced(parts, after):
     (piece,) = call(last_kernel, [out(parts[0].shape, BF)], *exchanged(parts, "y"), name="last")
     (piece,) = call(
-        total_kernel, [out(piece.shape, BF)], *spread(piece, "x"), after=after_x, name="total"
+        total_kernel, [out(piece.shape, BF)], *spread(piece, "x"), after=after, name="total"
     )
     return piece
 
@@ -629,8 +672,8 @@
     weights, sums, totals = [], [], []
     for s, q in enumerate(queries):
         others = (*totals, pos) if s == SIDE - 1 else ()
-        w, total, pack = call(
-            functools.partial(scores_kernel, len(others)),
+        w, grad, total = call(
+            scores_kernel,
             [
                 out((seqlen, SIDE * count), BF),
                 out((seqlen, width), F32 if s == 0 else BF),
@@ -644,13 +687,18 @@
             name="scores",
         )
         weights.append(w)
-        sums.append(total)
-        totals.append(pack)
+        sums.append(grad)
+        totals.append(total)
     sums[1:] = across(sums[1:], "queries")
+    pack = totals[-1]
     packs = [pack] + across([pack] * 3, "queries")
     pre, mixed, output = call(
         again_kernel,
-        [out((seqlen, 4 * width), F32), out((seqlen, width), F32), out((seqlen, width), F32)],
+        [
+            out((seqlen, 4 * width), F32),
+            out((seqlen, width), F32),
+            out((seqlen, width), F32),
+        ],
         seq_len,
         history,
         in_weight,
@@ -660,11 +708,11 @@
         after=(pack,),
         name="layer_again",
     )
-    *neg_parts, loss, factor = call(
+    half = out((count, width // 2), BF)
+    pair = out((2, count, width // 2), BF)
+    own_sum, first, second, third, last, loss, factor = call(
         neg_kernel,
-        [out((count, width), F32)]
-        + [out((count, width), BF)] * (SIDE - 1)
-        + [out((1, 1), F32), out((seqlen, 1), F32)],
+        [out((count, width), F32), pair, pair, half, half, out((1, 1), F32), out((seqlen, 1), F32)],
         seq_len,
         *packs,
         *queries,
@@ -674,7 +722,6 @@
         after=(output,),
         name="negative_sums",
     )
-    sent = across(neg_parts[1:], "negatives")
     row_grad, keep, send = call(
         backward_kernel,
         [
@@ -714,11 +761,15 @@
     arrived = lax.all_to_all(
         going.reshape(devices, SLOTS, width), AXES, split_axis=0, concat_axis=0, tiled=True
     ).reshape(devices * SLOTS, width)
-    piece = reduced(at, z_parts, (*sent,), (arrived,))
-    table_grad = table_grad_of(
-        asked.reshape(1, devices * SLOTS), arrived, neg_rows, own_rows, [neg_parts[0], *sent], owned
-    )
-    in_grad, out_grad = gathered(at, piece, (table_grad,))
+    first, second = square(first, "x"), square(second, "y")
+    third, last = call(turn_kernel, [half, half], third, first, last, second, name="turn")
+    third, last = square(third, "y"), square(last, "x")
+    y_first = scatter(at, 1, z_parts, (first, second))
+    piece = reduced(y_first, (third, last, arrived))
+    table_grad, table_done = table_grad_of(
+        asked.reshape(1, devices * SLOTS), arrived, neg_rows, own_rows, (own_sum, first, second, third, last), owned
+    )
+    in_grad, out_grad = gathered(at, piece, (table_done,))
     return (loss.reshape(1), in_grad, out_grad, table_grad)
 
 

time: 207 us -> 197 us (0.952)
  waiting for transfers between devices: 61 us -> 51.3 us
    ppermute x15 -> x12, waiting for transfers between devices: 28.3 us -> 4.24 us  [across(): lax.ppermute(v, 'member', [(m, m ^ mask) for m in range(SIDE * SIDE)])]
    ppermute x0 -> x4, waiting for transfers between devices: none -> 13.1 us  [square(): lax.ppermute(value, 'member', [(m, m ^ step) for m in range(SIDE * SIDE)])]
    ppermute x0 -> x4, starting transfers between devices: none -> 7.99 us  [square(): lax.ppermute(value, 'member', [(m, m ^ step) for m in range(SIDE * SIDE)])]
    ppermute x15 -> x12, starting transfers between devices: 24.2 us -> 19.1 us  [across(): lax.ppermute(v, 'member', [(m, m ^ mask) for m in range(SIDE * SIDE)])]
    pallas_call x18 -> x19, Pallas kernels: 40.8 us -> 40 us  [call(): pl.pallas_call(body, out_shape=outs, in_specs=in_specs, out_specs=[pl.Blo...]
    unnamed x68 -> x78, local copies, waits for them, and re-layouts: 14.7 us -> 14.1 us
  transfers between devices with their start and end apart: 34 -> 35, of which waited for: 15 -> 16; matrix products, arithmetic and copies ran while one was open for 1% -> 1% of each run, Pallas kernels for 14% -> 15%
where the time goes in v2:
time: 197 us; the launch traced here: 196 us
  starting transfers between devices  65.9 us (33%)
  waiting for transfers between devices  51.3 us (26%)
  Pallas kernels  45.4 us (23%)
  blocking collectives  15.8 us (8%)
  local copies, waits for them, and re-layouts  14.7 us (7%)
  between operations  2.05 us (1%)
    pallas_call x19, Pallas kernels, call(): pl.pallas_call(body, out_shape=outs, in_specs=in_specs, out_specs=[pl.Blo...  40 us
    ppermute x17, starting transfers between devices, shift_by(): return lax.ppermute(value, name, pairs)  24 us
    ppermute x17, waiting for transfers between devices, shift_by(): return lax.ppermute(value, name, pairs)  20.4 us
    ppermute x12, starting transfers between devices, across(): lax.ppermute(v, 'member', [(m, m ^ mask) for m in range(SIDE * SIDE)])  19.1 us
    all_to_all x1, blocking collectives, local(): lax.all_to_all(requests, AXES, split_axis=0, concat_axis=0, tiled=True)  15.8 us
    unnamed x78, local copies, waits for them, and re-layouts  14.1 us
    all_to_all x1, waiting for transfers between devices, local(): lax.all_to_all(found.reshape(devices, SLOTS, width), AXES, split_axis=0,...  13.5 us
    ppermute x4, waiting for transfers between devices, square(): lax.ppermute(value, 'member', [(m, m ^ step) for m in range(SIDE * SIDE)])  13.1 us
  transfers between devices with their start and end apart: 35, of which 16 were waited for; matrix products, arithmetic and copies ran while one was open for 1% of the time, Pallas kernels for 15%

profile of v2, /device:TPU:1, one launch (start us, length us, event | category | flops | bytes accessed | tf_op | source)
XLA Modules:
  0.0 196.0 jit_solution(17268856900345431334)
XLA Ops:
  5.3 3.6 %collective-permute-start.1 = (bf16[512,512]{1,0:T(8,128)(2,1)S(1)}, bf16[512,512]{1,0:T(8,128)(2,1)S(1)}, u32[]{:S(2)}, u32[]{:S(2)}) collective-permute-start(bf16[512,512]{1,0:T(8,128)(2,1)S(1)} %get-tuple-element.50.refs_2_.refs_1_), channel_id=1, source_target_pairs={{0,12},{1,13},{2,14},{3,15},{4,8},{5,9},{6,10},{7,11},{8,4},{9,5},... | collective-permute-start | bytes 1572872 | tf_op jit(solution)/shard_map/ppermute | solution.py:565
  12.2 15.8 %all_to_all.21 = s32[128,1,8]{2,1,0:T(1,128)S(1)} all-to-all(s32[128,1,8]{2,1,0:T(1,128)S(1)} %bitcast.24), channel_id=1, replica_groups=mesh['group'=8,'member'=16] {'group','member'}, dimensions={0} | all-to-all | bytes 8192 | tf_op jit(solution)/shard_map/all_to_all | solution.py:645
  28.1 3.2 %find_rows.1 = bf16[1024,512]{1,0:T(8,128)(2,1)S(1)} custom-call(s32[128,8]{1,0:T(8,128)S(1)} %bitcast.23, bf16[2048,512]{1,0:T(8,128)(2,1)S(1)} %copy-done.23, bf16[512,512]{1,0:T(8,128)(2,1)S(1)} %collective-permute-done.refs_2_, bf16[512,512]{1,0:T(8,128)(2,1)S(1)} %collective-permute-done.1.refs_3_), custom_call_target="tpu_custom_call" | custom-call | flops 2147483648 | bytes 3149824 | tf_op jit(solution)/shard_map/find_rows/pallas_call | solution.py:140
  32.2 7.4 %all-to-all-start.1 = ((bf16[128,8,512]{2,1,0:T(8,128)(2,1)}), bf16[128,8,512]{2,1,0:T(8,128)(2,1)S(1)}, u32[]{:S(2)}, u32[]{:S(2)}) async-start(bf16[128,8,512]{2,1,0:T(8,128)(2,1)} %bitcast.18), calls=%async_computation.1 | async-start | bytes 2097152 | tf_op jit(solution)/shard_map/all_to_all | solution.py:655
  39.6 4.9 %collective-permute-start.3 = (bf16[512,512]{1,0:T(8,128)(2,1)}, bf16[512,512]{1,0:T(8,128)(2,1)}, u32[]{:S(2)}, u32[]{:S(2)}) collective-permute-start(bf16[512,512]{1,0:T(8,128)(2,1)} %copy-done.4), channel_id=1, source_target_pairs={{0,15},{1,14},{2,13},{3,12},{4,11},{5,10},{6,9},{7,8},{8,7},{9,6},... | collective-permute-start | bytes 1572872 | tf_op jit(solution)/shard_map/ppermute | solution.py:565
  45.2 13.5 %all-to-all-done.1 = bf16[128,8,512]{2,1,0:T(8,128)(2,1)S(1)} async-done(((bf16[128,8,512]{2,1,0:T(8,128)(2,1)}), bf16[128,8,512]{2,1,0:T(8,128)(2,1)S(1)}, u32[]{:S(2)}, u32[]{:S(2)}) %all-to-all-start.1) | async-done | bytes 1048608 | tf_op jit(solution)/shard_map/all_to_all | solution.py:655
  60.6 3.2 %forward.1 = (bf16[256,512]{1,0:T(8,128)(2,1)S(1)}, bf16[256,512]{1,0:T(8,128)(2,1)}, f32[8,256]{1,0:T(8,128)S(1)}) custom-call(s32[1]{0:T(128)S(6)} %copy.12.refs_0_, bf16[1024,512]{1,0:T(8,128)(2,1)S(1)} %bitcast.17, s32[256,1]{1,0:T(8,128)S(1)} %copy-done.18, bf16[512,2048]{1,0:T(8,128)(2,1)S(1)} %copy-done, bf16[512,512]{1,0:T(8,128)(2,1)S(1)} %copy-done.2), custom_call_target="tpu_custom_call" | custom-call | flops 1073741824 | bytes 4203524 | tf_op jit(solution)/shard_map/forward/pallas_call | solution.py:140
  70.2 2.7 %scores.4 = (bf16[256,2048]{1,0:T(8,128)(2,1)S(1)}, f32[256,512]{1,0:T(8,128)S(1)}, f32[8,256]{1,0:T(8,128)S(1)}) custom-call(bf16[256,512]{1,0:T(8,128)(2,1)} %get-tuple-element.53.refs_0_.refs_5_, bf16[512,512]{1,0:T(8,128)(2,1)S(1)} %copy-done.5, bf16[512,512]{1,0:T(8,128)(2,1)S(1)} %copy-done.28, bf16[512,512]{1,0:T(8,128)(2,1)S(1)} %copy-done.25, ...), custom_call_target="tpu_custom_call" | custom-call | flops 1073741824 | bytes 3940352 | tf_op jit(solution)/shard_map/scores/pallas_call | solution.py:140
  73.0 2.6 %scores.6 = (bf16[256,2048]{1,0:T(8,128)(2,1)S(1)}, bf16[256,512]{1,0:T(8,128)(2,1)S(1)}, f32[8,256]{1,0:T(8,128)S(1)}) custom-call(bf16[256,512]{1,0:T(8,128)(2,1)S(1)} %collective-permute-done.5.refs_0_.refs_7_, bf16[512,512]{1,0:T(8,128)(2,1)S(1)} %copy-done.5, bf16[512,512]{1,0:T(8,128)(2,1)S(1)} %copy-done.28, bf16[512,512]{1,0:T(8,128)(2,1)S(1)} %copy-done.25, ...), custom_call_target="tpu_custom_call" | custom-call | flops 1073741824 | bytes 3678208 | tf_op jit(solution)/shard_map/scores/pallas_call | solution.py:140
  76.4 2.8 %scores.5 = (bf16[256,2048]{1,0:T(8,128)(2,1)S(1)}, bf16[256,512]{1,0:T(8,128)(2,1)S(1)}, f32[8,256]{1,0:T(8,128)S(1)}) custom-call(bf16[256,512]{1,0:T(8,128)(2,1)} %collective-permute-done.4.refs_0_.refs_6_, bf16[512,512]{1,0:T(8,128)(2,1)S(1)} %copy-done.5, bf16[512,512]{1,0:T(8,128)(2,1)S(1)} %copy-done.28, bf16[512,512]{1,0:T(8,128)(2,1)S(1)} %copy-done.25, ...), custom_call_target="tpu_custom_call" | custom-call | flops 1073741824 | bytes 3678208 | tf_op jit(solution)/shard_map/scores/pallas_call | solution.py:140
  79.3 2.7 %scores.7 = (bf16[256,2048]{1,0:T(8,128)(2,1)S(1)}, bf16[256,512]{1,0:T(8,128)(2,1)S(1)}, f32[8,256]{1,0:T(8,128)S(1)}) custom-call(bf16[256,512]{1,0:T(8,128)(2,1)S(1)} %collective-permute-done.2.refs_0_.refs_8_, bf16[512,512]{1,0:T(8,128)(2,1)S(1)} %copy-done.6, bf16[512,512]{1,0:T(8,128)(2,1)S(1)} %copy-done.29, bf16[512,512]{1,0:T(8,128)(2,1)S(1)} %copy-done.26, ...), custom_call_target="tpu_custom_call" | custom-call | flops 1073741824 | bytes 3710976 | tf_op jit(solution)/shard_map/scores/pallas_call | solution.py:140
  89.5 4.7 %negative_sums.1 = (f32[512,512]{1,0:T(8,128)S(1)}, bf16[2,512,256]{2,1,0:T(8,128)(2,1)}, bf16[2,512,256]{2,1,0:T(8,128)(2,1)S(1)}, bf16[512,256]{1,0:T(8,128)(2...) custom-call(s32[1]{0:T(128)S(6)} %copy.12.refs_0_, ...), custom_call_target="tpu_custom_call" | custom-call | flops 2147483648 | bytes 7898120 | tf_op jit(solution)/shard_map/negative_sums/pallas_call | solution.py:140
  94.2 3.6 %collective-permute-done.10.refs_5_ = bf16[256,512]{1,0:T(8,128)(2,1)S(1)} collective-permute-done((bf16[256,512]{1,0:T(8,128)(2,1)S(1)}, bf16[256,512]{1,0:T(8,128)(2,1)S(1)}, u32[]{:S(2)}, u32[]{:S(2)}) %collective-permute-start.10) | collective-permute-done | bytes 262176 | tf_op jit(solution)/shard_map/ppermute | solution.py:565
  97.9 5.9 %backward.1 = (bf16[256,512]{1,0:T(8,128)(2,1)S(1)}, bf16[256,2560]{1,0:T(8,128)(2,1)S(1)}, bf16[256,2560]{1,0:T(8,128)(2,1)}) custom-call(s32[1]{0:T(128)S(6)} %copy.12.refs_0_, s32[4]{0:T(128)S(1)} %pad_add_fusion.refs_1_.refs_0_, f32[256,1]{1,0:T(8,128)S(1)} %get-tuple-element.67.refs_2_, f32[256,512]{1,0:T(8,128)S(1)} %get-tuple-element.55.refs_5_.refs_9_.refs_3_, ...), custom_call_target="tpu_custom_call" | custom-call | flops 1879048192 | bytes 10224660 | tf_op jit(solution)/shard_map/backward/pallas_call | solution.py:140
  108.0 7.5 %all-to-all-start.2 = ((bf16[128,8,512]{2,1,0:T(8,128)(2,1)}), bf16[128,8,512]{2,1,0:T(8,128)(2,1)S(1)}, u32[]{:S(2)}, u32[]{:S(2)}) async-start(bf16[128,8,512]{2,1,0:T(8,128)(2,1)} %bitcast.11), calls=%async_computation.2 | async-start | bytes 2097152 | tf_op jit(solution)/shard_map/all_to_all | solution.py:761
  115.5 2.7 %collective-permute-start.16 = (bf16[2,512,256]{2,1,0:T(8,128)(2,1)}, bf16[2,512,256]{2,1,0:T(8,128)(2,1)S(1)}, u32[]{:S(2)}, u32[]{:S(2)}) collective-permute-start(bf16[2,512,256]{2,1,0:T(8,128)(2,1)} %get-tuple-element.79), channel_id=1, source_target_pairs={{0,3},{1,2},{2,1},{3,0},{4,7},{5,6},{6,5},{7,4},{8,11},{9,10},{10,... | collective-permute-start | bytes 1572872 | tf_op jit(solution)/shard_map/ppermute | solution.py:558
  124.1 2.9 %collective-permute-start.14 = (bf16[64,2560]{1,0:T(8,128)(2,1)S(1)}, bf16[64,2560]{1,0:T(8,128)(2,1)S(1)}, u32[]{:S(2)}, u32[]{:S(2)}) collective-permute-start(bf16[64,2560]{1,0:T(8,128)(2,1)S(1)} %get-tuple-element.77), channel_id=1, source_target_pairs={{0,64},{16,80},{32,96},{48,112},{64,0},{80,16},{96,32},{112,48},{1... | collective-permute-start | bytes 983048 | tf_op jit(solution)/shard_map/ppermute | solution.py:549
  128.0 12.7 %collective-permute-done.16.refs_5_.refs_1_.first_ref = bf16[2,512,256]{2,1,0:T(8,128)(2,1)S(1)} collective-permute-done((bf16[2,512,256]{2,1,0:T(8,128)(2,1)}, bf16[2,512,256]{2,1,0:T(8,128)(2,1)S(1)}, u32[]{:S(2)}, u32[]{:S(2)}) %collective-permute-start.16) | collective-permute-done | bytes 524320 | tf_op jit(solution)/shard_map/ppermute | solution.py:558
  157.8 3.0 %collective-permute-done.22.refs_2_ = bf16[16,2560]{1,0:T(8,128)(2,1)S(1)} collective-permute-done((bf16[16,2560]{1,0:T(8,128)(2,1)S(1)}, bf16[16,2560]{1,0:T(8,128)(2,1)S(1)}, u32[]{:S(2)}, u32[]{:S(2)}) %collective-permute-start.22) | collective-permute-done | bytes 81952 | tf_op jit(solution)/shard_map/ppermute | solution.py:549
  178.0 5.4 %table_grad.1 = (f32[2048,512]{1,0:T(8,128)}, f32[8,128]{1,0:T(8,128)S(1)}) custom-call(s32[1,1024]{1,0:T(1,128)S(1)} %reshape.38.asked_ref, bf16[1024,512]{1,0:T(8,128)(2,1)S(1)} %bitcast.16, s32[1,512]{1,0:T(1,128)S(1)} %copy-done.34, bf16[512,512]{1,0:T(8,128)(2,1)S(1)} %copy-done.38, f32[512,512]{1,0:T(8,128)S(1)} %copy-done.36, ...), custom_call_target="tpu_custom_call" | custom-call | flops 3221225472 | bytes 4194304 | tf_op jit(solution)/shard_map/table_grad/pallas_call | solution.py:464
  183.4 3.5 %collective-permute-done.29.refs_1_ = bf16[4,16,2560]{2,1,0:T(8,128)(2,1)S(1)} collective-permute-done((bf16[4,16,2560]{2,1,0:T(8,128)(2,1)S(1)}, bf16[4,16,2560]{2,1,0:T(8,128)(2,1)S(1)}, u32[]{:S(2)}, u32[]{:S(2)}) %collective-permute-start.29) | collective-permute-done | bytes 327712 | tf_op jit(solution)/shard_map/ppermute | solution.py:549
  187.0 2.9 %collective-permute-start.32 = (bf16[16,16,2560]{2,1,0:T(8,128)(2,1)S(1)}, bf16[16,16,2560]{2,1,0:T(8,128)(2,1)S(1)}, u32[]{:S(2)}, u32[]{:S(2)}) collective-permute-start(bf16[16,16,2560]{2,1,0:T(8,128)(2,1)S(1)} %stack.21.refs_1_), channel_id=1, source_target_pairs={{0,16},{16,0},{32,48},{48,32},{64,80},{80,64},{96,112},{112,96},{1... | collective-permute-start | bytes 3932168 | tf_op jit(solution)/shard_map/ppermute | solution.py:549
  189.9 2.7 %collective-permute-done.32.refs_2_ = bf16[16,16,2560]{2,1,0:T(8,128)(2,1)S(1)} collective-permute-done((bf16[16,16,2560]{2,1,0:T(8,128)(2,1)S(1)}, bf16[16,16,2560]{2,1,0:T(8,128)(2,1)S(1)}, u32[]{:S(2)}, u32[]{:S(2)}) %collective-permute-start.32) | collective-permute-done | bytes 1310752 | tf_op jit(solution)/shard_map/ppermute | solution.py:549
  192.6 3.2 %place.1 = (f32[512,2048]{1,0:T(8,128)}, f32[512,512]{1,0:T(8,128)}) custom-call(s32[4]{0:T(128)S(1)} %pad_add_fusion.refs_1_.refs_0_, bf16[16,16,2560]{2,1,0:T(8,128)(2,1)S(1)} %stack.21.refs_1_, bf16[16,16,2560]{2,1,0:T(8,128)(2,1)S(1)} %collective-permute-done.32.refs_2_), custom_call_target="tpu_custom_call" | custom-call | bytes 7864336 | tf_op jit(solution)/shard_map/place/pallas_call | solution.py:140
  (150 shorter events, 70.9 us)
Async XLA Ops:
  5.3 22.7 %collective-permute-start.1 = (bf16[512,512]{1,0:T(8,128)(2,1)S(1)}, bf16[512,512]{1,0:T(8,128)(2,1)S(1)}, u32[]{:S(2)}, u32[]{:S(2)}) collective-permute-start(bf16[512,512]{1,0:T(8,128)(2,1)S(1)} %get-tuple-element.50.refs_2_.refs_1_), channel_id=1, source_target_pairs={{0,12},{1,13},{2,14},{3,15},{4,8},{5,9},{6,10},{7,11},{8,4},{9,5},... | collective-permute-start | bytes 1572872 | tf_op jit(solution)/shard_map/ppermute | solution.py:565
  8.9 19.1 %collective-permute-start = (bf16[512,512]{1,0:T(8,128)(2,1)S(1)}, bf16[512,512]{1,0:T(8,128)(2,1)S(1)}, u32[]{:S(2)}, u32[]{:S(2)}) collective-permute-start(bf16[512,512]{1,0:T(8,128)(2,1)S(1)} %get-tuple-element.50.refs_2_.refs_1_), channel_id=1, source_target_pairs={{0,3},{1,2},{2,1},{3,0},{4,7},{5,6},{6,5},{7,4},{8,11},{9,10},{10,... | collective-permute-start | bytes 1572872 | tf_op jit(solution)/shard_map/ppermute | solution.py:565
  32.2 26.4 %all-to-all-start.1 = ((bf16[128,8,512]{2,1,0:T(8,128)(2,1)}), bf16[128,8,512]{2,1,0:T(8,128)(2,1)S(1)}, u32[]{:S(2)}, u32[]{:S(2)}) async-start(bf16[128,8,512]{2,1,0:T(8,128)(2,1)} %bitcast.18), calls=%async_computation.1 | async-start | bytes 2097152 | tf_op jit(solution)/shard_map/all_to_all | solution.py:655
  39.6 27.5 %collective-permute-start.3 = (bf16[512,512]{1,0:T(8,128)(2,1)}, bf16[512,512]{1,0:T(8,128)(2,1)}, u32[]{:S(2)}, u32[]{:S(2)}) collective-permute-start(bf16[512,512]{1,0:T(8,128)(2,1)} %copy-done.4), channel_id=1, source_target_pairs={{0,15},{1,14},{2,13},{3,12},{4,11},{5,10},{6,9},{7,8},{8,7},{9,6},... | collective-permute-start | bytes 1572872 | tf_op jit(solution)/shard_map/ppermute | solution.py:565
  63.8 9.2 %collective-permute-start.5 = (bf16[256,512]{1,0:T(8,128)(2,1)}, bf16[256,512]{1,0:T(8,128)(2,1)S(1)}, u32[]{:S(2)}, u32[]{:S(2)}) collective-permute-start(bf16[256,512]{1,0:T(8,128)(2,1)} %get-tuple-element.53.refs_0_.refs_5_), channel_id=1, source_target_pairs={{0,4},{1,5},{2,6},{3,7},{4,0},{5,1},{6,2},{7,3},{8,12},{9,13},{10,... | collective-permute-start | bytes 786440 | tf_op jit(solution)/shard_map/ppermute | solution.py:565
  64.6 11.8 %collective-permute-start.4 = (bf16[256,512]{1,0:T(8,128)(2,1)}, bf16[256,512]{1,0:T(8,128)(2,1)}, u32[]{:S(2)}, u32[]{:S(2)}) collective-permute-start(bf16[256,512]{1,0:T(8,128)(2,1)} %get-tuple-element.53.refs_0_.refs_5_), channel_id=1, source_target_pairs={{0,1},{1,0},{2,3},{3,2},{4,5},{5,4},{6,7},{7,6},{8,9},{9,8},{10,11... | collective-permute-start | bytes 786440 | tf_op jit(solution)/shard_map/ppermute | solution.py:565
  64.9 14.3 %collective-permute-start.2 = (bf16[256,512]{1,0:T(8,128)(2,1)}, bf16[256,512]{1,0:T(8,128)(2,1)S(1)}, u32[]{:S(2)}, u32[]{:S(2)}) collective-permute-start(bf16[256,512]{1,0:T(8,128)(2,1)} %get-tuple-element.53.refs_0_.refs_5_), channel_id=1, source_target_pairs={{0,5},{1,4},{2,7},{3,6},{4,1},{5,0},{6,3},{7,2},{8,13},{9,12},{10,... | collective-permute-start | bytes 786440 | tf_op jit(solution)/shard_map/ppermute | solution.py:565
  82.3 7.2 %collective-permute-start.7 = (f32[8,256]{1,0:T(8,128)S(1)}, f32[8,256]{1,0:T(8,128)S(1)}, u32[]{:S(2)}, u32[]{:S(2)}) collective-permute-start(f32[8,256]{1,0:T(8,128)S(1)} %get-tuple-element.59.refs_4_.refs_1_), channel_id=1, source_target_pairs={{0,4},{1,5},{2,6},{3,7},{4,0},{5,1},{6,2},{7,3},{8,12},{9,13},{10,... | collective-permute-start | bytes 24584 | tf_op jit(solution)/shard_map/ppermute | solution.py:565
  83.5 6.0 %collective-permute-start.6 = (f32[8,256]{1,0:T(8,128)S(1)}, f32[8,256]{1,0:T(8,128)S(1)}, u32[]{:S(2)}, u32[]{:S(2)}) collective-permute-start(f32[8,256]{1,0:T(8,128)S(1)} %get-tuple-element.59.refs_4_.refs_1_), channel_id=1, source_target_pairs={{0,1},{1,0},{2,3},{3,2},{4,5},{5,4},{6,7},{7,6},{8,9},{9,8},{10,11... | collective-permute-start | bytes 24584 | tf_op jit(solution)/shard_map/ppermute | solution.py:565
  84.8 13.1 %collective-permute-start.10 = (bf16[256,512]{1,0:T(8,128)(2,1)S(1)}, bf16[256,512]{1,0:T(8,128)(2,1)S(1)}, u32[]{:S(2)}, u32[]{:S(2)}) collective-permute-start(bf16[256,512]{1,0:T(8,128)(2,1)S(1)} %get-tuple-element.69), channel_id=1, source_target_pairs={{0,4},{1,5},{2,6},{3,7},{4,0},{5,1},{6,2},{7,3},{8,12},{9,13},{10,... | collective-permute-start | bytes 786440 | tf_op jit(solution)/shard_map/ppermute | solution.py:565
  84.9 12.9 %collective-permute-start.11 = (bf16[256,512]{1,0:T(8,128)(2,1)S(1)}, bf16[256,512]{1,0:T(8,128)(2,1)S(1)}, u32[]{:S(2)}, u32[]{:S(2)}) collective-permute-start(bf16[256,512]{1,0:T(8,128)(2,1)S(1)} %get-tuple-element.70), channel_id=1, source_target_pairs={{0,5},{1,4},{2,7},{3,6},{4,1},{5,0},{6,3},{7,2},{8,13},{9,12},{10,... | collective-permute-start | bytes 786440 | tf_op jit(solution)/shard_map/ppermute | solution.py:565
  86.1 11.7 %collective-permute-start.9 = (bf16[256,512]{1,0:T(8,128)(2,1)S(1)}, bf16[256,512]{1,0:T(8,128)(2,1)S(1)}, u32[]{:S(2)}, u32[]{:S(2)}) collective-permute-start(bf16[256,512]{1,0:T(8,128)(2,1)S(1)} %get-tuple-element.68), channel_id=1, source_target_pairs={{0,1},{1,0},{2,3},{3,2},{4,5},{5,4},{6,7},{7,6},{8,9},{9,8},{10,11... | collective-permute-start | bytes 786440 | tf_op jit(solution)/shard_map/ppermute | solution.py:565
  103.8 16.9 %collective-permute-start.12 = (bf16[256,2560]{1,0:T(8,128)(2,1)}, bf16[256,2560]{1,0:T(8,128)(2,1)}, u32[]{:S(2)}, u32[]{:S(2)}) collective-permute-start(bf16[256,2560]{1,0:T(8,128)(2,1)} %get-tuple-element.74), channel_id=1, source_target_pairs={{0,16},{16,0},{32,48},{48,32},{64,80},{80,64},{96,112},{112,96},{1... | collective-permute-start | bytes 3932168 | tf_op jit(solution)/shard_map/ppermute | solution.py:549
  108.0 49.8 %all-to-all-start.2 = ((bf16[128,8,512]{2,1,0:T(8,128)(2,1)}), bf16[128,8,512]{2,1,0:T(8,128)(2,1)S(1)}, u32[]{:S(2)}, u32[]{:S(2)}) async-start(bf16[128,8,512]{2,1,0:T(8,128)(2,1)} %bitcast.11), calls=%async_computation.2 | async-start | bytes 2097152 | tf_op jit(solution)/shard_map/all_to_all | solution.py:761
  115.5 25.2 %collective-permute-start.16 = (bf16[2,512,256]{2,1,0:T(8,128)(2,1)}, bf16[2,512,256]{2,1,0:T(8,128)(2,1)S(1)}, u32[]{:S(2)}, u32[]{:S(2)}) collective-permute-start(bf16[2,512,256]{2,1,0:T(8,128)(2,1)} %get-tuple-element.79), channel_id=1, source_target_pairs={{0,3},{1,2},{2,1},{3,0},{4,7},{5,6},{6,5},{7,4},{8,11},{9,10},{10,... | collective-permute-start | bytes 1572872 | tf_op jit(solution)/shard_map/ppermute | solution.py:558
  118.2 22.9 %collective-permute-start.17 = (bf16[2,512,256]{2,1,0:T(8,128)(2,1)}, bf16[2,512,256]{2,1,0:T(8,128)(2,1)S(1)}, u32[]{:S(2)}, u32[]{:S(2)}) collective-permute-start(bf16[2,512,256]{2,1,0:T(8,128)(2,1)} %copy-done.30), channel_id=1, source_target_pairs={{0,12},{1,13},{2,14},{3,15},{4,8},{5,9},{6,10},{7,11},{8,4},{9,5},... | collective-permute-start | bytes 1572872 | tf_op jit(solution)/shard_map/ppermute | solution.py:558
  122.6 21.4 %collective-permute-start.13 = (bf16[64,2560]{1,0:T(8,128)(2,1)S(1)}, bf16[64,2560]{1,0:T(8,128)(2,1)S(1)}, u32[]{:S(2)}, u32[]{:S(2)}) collective-permute-start(bf16[64,2560]{1,0:T(8,128)(2,1)S(1)} %get-tuple-element.76), channel_id=1, source_target_pairs={{0,32},{16,48},{32,64},{48,80},{64,96},{80,112},{96,0},{112,16},{1... | collective-permute-start | bytes 983048 | tf_op jit(solution)/shard_map/ppermute | solution.py:549
  124.1 22.0 %collective-permute-start.14 = (bf16[64,2560]{1,0:T(8,128)(2,1)S(1)}, bf16[64,2560]{1,0:T(8,128)(2,1)S(1)}, u32[]{:S(2)}, u32[]{:S(2)}) collective-permute-start(bf16[64,2560]{1,0:T(8,128)(2,1)S(1)} %get-tuple-element.77), channel_id=1, source_target_pairs={{0,64},{16,80},{32,96},{48,112},{64,0},{80,16},{96,32},{112,48},{1... | collective-permute-start | bytes 983048 | tf_op jit(solution)/shard_map/ppermute | solution.py:549
  127.0 19.1 %collective-permute-start.15 = (bf16[64,2560]{1,0:T(8,128)(2,1)S(1)}, bf16[64,2560]{1,0:T(8,128)(2,1)S(1)}, u32[]{:S(2)}, u32[]{:S(2)}) collective-permute-start(bf16[64,2560]{1,0:T(8,128)(2,1)S(1)} %get-tuple-element.78), channel_id=1, source_target_pairs={{0,96},{16,112},{32,0},{48,16},{64,32},{80,48},{96,64},{112,80},{1... | collective-permute-start | bytes 983048 | tf_op jit(solution)/shard_map/ppermute | solution.py:549
  141.2 16.6 %collective-permute-start.24 = (bf16[512,256]{1,0:T(8,128)(2,1)S(1)}, bf16[512,256]{1,0:T(8,128)(2,1)S(1)}, u32[]{:S(2)}, u32[]{:S(2)}) collective-permute-start(bf16[512,256]{1,0:T(8,128)(2,1)S(1)} %get-tuple-element.87), channel_id=1, source_target_pairs={{0,12},{1,13},{2,14},{3,15},{4,8},{5,9},{6,10},{7,11},{8,4},{9,5},... | collective-permute-start | bytes 786440 | tf_op jit(solution)/shard_map/ppermute | solution.py:558
  143.6 14.1 %collective-permute-start.25 = (bf16[512,256]{1,0:T(8,128)(2,1)S(1)}, bf16[512,256]{1,0:T(8,128)(2,1)S(1)}, u32[]{:S(2)}, u32[]{:S(2)}) collective-permute-start(bf16[512,256]{1,0:T(8,128)(2,1)S(1)} %get-tuple-element.88), channel_id=1, source_target_pairs={{0,3},{1,2},{2,1},{3,0},{4,7},{5,6},{6,5},{7,4},{8,11},{9,10},{10,... | collective-permute-start | bytes 786440 | tf_op jit(solution)/shard_map/ppermute | solution.py:558
  169.9 13.5 %collective-permute-start.31 = (bf16[4,16,2560]{2,1,0:T(8,128)(2,1)S(1)}, bf16[4,16,2560]{2,1,0:T(8,128)(2,1)S(1)}, u32[]{:S(2)}, u32[]{:S(2)}) collective-permute-start(bf16[4,16,2560]{2,1,0:T(8,128)(2,1)S(1)} %pad_maximum_fusion.refs_0_), channel_id=1, source_target_pairs={{0,96},{16,112},{32,0},{48,16},{64,32},{80,48},{96,64},{112,80},{1... | collective-permute-start | bytes 983048 | tf_op jit(solution)/shard_map/ppermute | solution.py:549
  171.1 12.3 %collective-permute-start.30 = (bf16[4,16,2560]{2,1,0:T(8,128)(2,1)S(1)}, bf16[4,16,2560]{2,1,0:T(8,128)(2,1)S(1)}, u32[]{:S(2)}, u32[]{:S(2)}) collective-permute-start(bf16[4,16,2560]{2,1,0:T(8,128)(2,1)S(1)} %pad_maximum_fusion.refs_0_), channel_id=1, source_target_pairs={{0,64},{16,80},{32,96},{48,112},{64,0},{80,16},{96,32},{112,48},{1... | collective-permute-start | bytes 983048 | tf_op jit(solution)/shard_map/ppermute | solution.py:549
  172.1 14.9 %collective-permute-start.29 = (bf16[4,16,2560]{2,1,0:T(8,128)(2,1)S(1)}, bf16[4,16,2560]{2,1,0:T(8,128)(2,1)S(1)}, u32[]{:S(2)}, u32[]{:S(2)}) collective-permute-start(bf16[4,16,2560]{2,1,0:T(8,128)(2,1)S(1)} %pad_maximum_fusion.refs_0_), channel_id=1, source_target_pairs={{0,32},{16,48},{32,64},{48,80},{64,96},{80,112},{96,0},{112,16},{1... | collective-permute-start | bytes 983048 | tf_op jit(solution)/shard_map/ppermute | solution.py:549
  (50 other events, 394.8 us)

commit v3 on v2

--- a/solution.py
+++ b/solution.py
@@ -349,9 +349,9 @@
 
 def backward_kernel(
     len_ref, at_ref, factor_ref, sum0, sum1, sum2, sum3, hist_ref, pre_ref, mixed_ref, output_ref,
-    in_ref, out_ref,
-    row_ref, keep_ref, send_ref,
-    normed_ref, gated_ref, dpre_ref,
+    in_ref, out_ref, slots_ref,
+    going_ref, keep_ref, send_ref,
+    normed_ref, gated_ref, dpre_ref, row_ref,
 ):
     length = len_ref[0]
     core = at_ref[3]
@@ -424,10 +424,7 @@
         ref[:, 4 * width :] = mm_tn(gated_ref[:, rows], output_bf).astype(BF)
     d_normed = mm_nt(dpre_ref[...], in_ref[...]).astype(BF).astype(F32)
     row_ref[...] = (output_grad + norm_back(normed, scale, d_normed) + shifted).astype(BF)
-
-
-def going_kernel(slots_ref, row_ref, going_ref):
-    pick = ones_where(slots_ref[...] == iota((row_ref.shape[0], going_ref.shape[0]), 1))
+    pick = ones_where(slots_ref[...] == iota((seqlen, going_ref.shape[0]), 1))
     going_ref[...] = mm_tn(pick, row_ref[...]).astype(BF)
 
 
@@ -722,10 +719,10 @@
         after=(output,),
         name="negative_sums",
     )
-    row_grad, keep, send = call(
+    going, keep, send = call(
         backward_kernel,
         [
-            out((seqlen, width), BF),
+            out((devices * SLOTS, width), BF),
             out((width // 2, 5 * width), BF),
             out((width // 2, 5 * width), BF),
         ],
@@ -739,25 +736,19 @@
         output,
         in_weight,
         out_weight,
+        slots,
         smem=(0, 1),
         scratch=[
             pltpu.VMEM((seqlen, width), BF),
             pltpu.VMEM((seqlen, width), BF),
             pltpu.VMEM((seqlen, 4 * width), BF),
+            pltpu.VMEM((seqlen, width), BF),
         ],
         flops=2 * seqlen * width * 14 * width,
         name="backward",
     )
     got = shift_by(send, "core", 1)
     z_parts = exchanged(scatter(at, 2, [keep, got]), "z")
-    (going,) = call(
-        going_kernel,
-        [out((devices * SLOTS, width), BF)],
-        slots,
-        row_grad,
-        flops=2 * devices * SLOTS * seqlen * width,
-        name="going",
-    )
     arrived = lax.all_to_all(
         going.reshape(devices, SLOTS, width), AXES, split_axis=0, concat_axis=0, tiled=True
     ).reshape(devices * SLOTS, width)

time: 197 us -> 196 us (level)
    pallas_call x19 -> x18, Pallas kernels: 40 us -> 38.3 us  [call(): pl.pallas_call(body, out_shape=outs, in_specs=in_specs, out_specs=[pl.Blo...]
    unnamed x78 -> x80, local copies, waits for them, and re-layouts: 14.1 us -> 15 us
  transfers between devices with their start and end apart: 35 -> 35, of which waited for: 16 -> 17; matrix products, arithmetic and copies ran while one was open for 1% -> 1% of each run, Pallas kernels for 15% -> 14%
where the time goes in v3:
time: 196 us; the launch traced here: 195 us
  starting transfers between devices  64.6 us (33%)
  waiting for transfers between devices  52.4 us (27%)
  Pallas kernels  43.7 us (22%)
  blocking collectives  15.8 us (8%)
  local copies, waits for them, and re-layouts  15.6 us (8%)
  between operations  2.04 us (1%)
    pallas_call x18, Pallas kernels, call(): pl.pallas_call(body, out_shape=outs, in_specs=in_specs, out_specs=[pl.Blo...  38.3 us
    ppermute x17, starting transfers between devices, shift_by(): return lax.ppermute(value, name, pairs)  23 us
    ppermute x17, waiting for transfers between devices, shift_by(): return lax.ppermute(value, name, pairs)  21.6 us
    ppermute x12, starting transfers between devices, across(): lax.ppermute(v, 'member', [(m, m ^ mask) for m in range(SIDE * SIDE)])  19.1 us
    all_to_all x1, blocking collectives, local(): lax.all_to_all(requests, AXES, split_axis=0, concat_axis=0, tiled=True)  15.8 us
    unnamed x80, local copies, waits for them, and re-layouts  15 us
    all_to_all x1, waiting for transfers between devices, local(): lax.all_to_all(found.reshape(devices, SLOTS, width), AXES, split_axis=0,...  13.5 us
    ppermute x4, waiting for transfers between devices, square(): lax.ppermute(value, 'member', [(m, m ^ step) for m in range(SIDE * SIDE)])  13.1 us
  transfers between devices with their start and end apart: 35, of which 17 were waited for; matrix products, arithmetic and copies ran while one was open for 1% of the time, Pallas kernels for 14%

profile of v3, /device:TPU:1, one launch (start us, length us, event | category | flops | bytes accessed | tf_op | source)
XLA Modules:
  0.0 195.2 jit_solution(2211867049199817073)
XLA Ops:
  5.3 3.6 %collective-permute-start.1 = (bf16[512,512]{1,0:T(8,128)(2,1)S(1)}, bf16[512,512]{1,0:T(8,128)(2,1)S(1)}, u32[]{:S(2)}, u32[]{:S(2)}) collective-permute-start(bf16[512,512]{1,0:T(8,128)(2,1)S(1)} %get-tuple-element.50.refs_2_.refs_1_), channel_id=1, source_target_pairs={{0,12},{1,13},{2,14},{3,15},{4,8},{5,9},{6,10},{7,11},{8,4},{9,5},... | collective-permute-start | bytes 1572872 | tf_op jit(solution)/shard_map/ppermute | solution.py:562
  12.2 15.8 %all_to_all.21 = s32[128,1,8]{2,1,0:T(1,128)S(1)} all-to-all(s32[128,1,8]{2,1,0:T(1,128)S(1)} %bitcast.25), channel_id=1, replica_groups=mesh['group'=8,'member'=16] {'group','member'}, dimensions={0} | all-to-all | bytes 8192 | tf_op jit(solution)/shard_map/all_to_all | solution.py:642
  28.1 3.2 %find_rows.1 = bf16[1024,512]{1,0:T(8,128)(2,1)S(1)} custom-call(s32[128,8]{1,0:T(8,128)S(1)} %bitcast.24, bf16[2048,512]{1,0:T(8,128)(2,1)S(1)} %copy-done.24, bf16[512,512]{1,0:T(8,128)(2,1)S(1)} %collective-permute-done.refs_2_, bf16[512,512]{1,0:T(8,128)(2,1)S(1)} %collective-permute-done.1.refs_3_), custom_call_target="tpu_custom_call" | custom-call | flops 2147483648 | bytes 3149824 | tf_op jit(solution)/shard_map/find_rows/pallas_call | solution.py:140
  32.2 7.4 %all-to-all-start.1 = ((bf16[128,8,512]{2,1,0:T(8,128)(2,1)}), bf16[128,8,512]{2,1,0:T(8,128)(2,1)S(1)}, u32[]{:S(2)}, u32[]{:S(2)}) async-start(bf16[128,8,512]{2,1,0:T(8,128)(2,1)} %bitcast.19), calls=%async_computation.1 | async-start | bytes 2097152 | tf_op jit(solution)/shard_map/all_to_all | solution.py:652
  39.6 4.9 %collective-permute-start.3 = (bf16[512,512]{1,0:T(8,128)(2,1)}, bf16[512,512]{1,0:T(8,128)(2,1)}, u32[]{:S(2)}, u32[]{:S(2)}) collective-permute-start(bf16[512,512]{1,0:T(8,128)(2,1)} %copy-done.5), channel_id=1, source_target_pairs={{0,15},{1,14},{2,13},{3,12},{4,11},{5,10},{6,9},{7,8},{8,7},{9,6},... | collective-permute-start | bytes 1572872 | tf_op jit(solution)/shard_map/ppermute | solution.py:562
  45.2 13.5 %all-to-all-done.1 = bf16[128,8,512]{2,1,0:T(8,128)(2,1)S(1)} async-done(((bf16[128,8,512]{2,1,0:T(8,128)(2,1)}), bf16[128,8,512]{2,1,0:T(8,128)(2,1)S(1)}, u32[]{:S(2)}, u32[]{:S(2)}) %all-to-all-start.1) | async-done | bytes 1048608 | tf_op jit(solution)/shard_map/all_to_all | solution.py:652
  60.6 3.2 %forward.1 = (bf16[256,512]{1,0:T(8,128)(2,1)S(1)}, bf16[256,512]{1,0:T(8,128)(2,1)}, f32[8,256]{1,0:T(8,128)S(1)}) custom-call(s32[1]{0:T(128)S(6)} %copy.12.refs_0_, bf16[1024,512]{1,0:T(8,128)(2,1)S(1)} %bitcast.18, s32[256,1]{1,0:T(8,128)S(1)} %copy-done.19, bf16[512,2048]{1,0:T(8,128)(2,1)S(1)} %copy-done, bf16[512,512]{1,0:T(8,128)(2,1)S(1)} %copy-done.3), custom_call_target="tpu_custom_call" | custom-call | flops 1073741824 | bytes 4203524 | tf_op jit(solution)/shard_map/forward/pallas_call | solution.py:140
  70.2 2.7 %scores.4 = (bf16[256,2048]{1,0:T(8,128)(2,1)S(1)}, f32[256,512]{1,0:T(8,128)S(1)}, f32[8,256]{1,0:T(8,128)S(1)}) custom-call(bf16[256,512]{1,0:T(8,128)(2,1)} %get-tuple-element.53.refs_0_.refs_5_, bf16[512,512]{1,0:T(8,128)(2,1)S(1)} %copy-done.6, bf16[512,512]{1,0:T(8,128)(2,1)S(1)} %copy-done.29, bf16[512,512]{1,0:T(8,128)(2,1)S(1)} %copy-done.26, ...), custom_call_target="tpu_custom_call" | custom-call | flops 1073741824 | bytes 3940352 | tf_op jit(solution)/shard_map/scores/pallas_call | solution.py:140
  73.0 2.6 %scores.6 = (bf16[256,2048]{1,0:T(8,128)(2,1)S(1)}, bf16[256,512]{1,0:T(8,128)(2,1)S(1)}, f32[8,256]{1,0:T(8,128)S(1)}) custom-call(bf16[256,512]{1,0:T(8,128)(2,1)S(1)} %collective-permute-done.5.refs_0_.refs_7_, bf16[512,512]{1,0:T(8,128)(2,1)S(1)} %copy-done.6, bf16[512,512]{1,0:T(8,128)(2,1)S(1)} %copy-done.29, bf16[512,512]{1,0:T(8,128)(2,1)S(1)} %copy-done.26, ...), custom_call_target="tpu_custom_call" | custom-call | flops 1073741824 | bytes 3678208 | tf_op jit(solution)/shard_map/scores/pallas_call | solution.py:140
  76.4 2.9 %scores.5 = (bf16[256,2048]{1,0:T(8,128)(2,1)S(1)}, bf16[256,512]{1,0:T(8,128)(2,1)S(1)}, f32[8,256]{1,0:T(8,128)S(1)}) custom-call(bf16[256,512]{1,0:T(8,128)(2,1)} %collective-permute-done.4.refs_0_.refs_6_, bf16[512,512]{1,0:T(8,128)(2,1)S(1)} %copy-done.6, bf16[512,512]{1,0:T(8,128)(2,1)S(1)} %copy-done.29, bf16[512,512]{1,0:T(8,128)(2,1)S(1)} %copy-done.26, ...), custom_call_target="tpu_custom_call" | custom-call | flops 1073741824 | bytes 3678208 | tf_op jit(solution)/shard_map/scores/pallas_call | solution.py:140
  79.3 2.7 %scores.7 = (bf16[256,2048]{1,0:T(8,128)(2,1)S(1)}, bf16[256,512]{1,0:T(8,128)(2,1)S(1)}, f32[8,256]{1,0:T(8,128)S(1)}) custom-call(bf16[256,512]{1,0:T(8,128)(2,1)S(1)} %collective-permute-done.2.refs_0_.refs_8_, bf16[512,512]{1,0:T(8,128)(2,1)S(1)} %copy-done.7, bf16[512,512]{1,0:T(8,128)(2,1)S(1)} %copy-done.30, bf16[512,512]{1,0:T(8,128)(2,1)S(1)} %copy-done.27, ...), custom_call_target="tpu_custom_call" | custom-call | flops 1073741824 | bytes 3710976 | tf_op jit(solution)/shard_map/scores/pallas_call | solution.py:140
  89.5 4.7 %negative_sums.1 = (f32[512,512]{1,0:T(8,128)S(1)}, bf16[2,512,256]{2,1,0:T(8,128)(2,1)}, bf16[2,512,256]{2,1,0:T(8,128)(2,1)S(1)}, bf16[512,256]{1,0:T(8,128)(2...) custom-call(s32[1]{0:T(128)S(6)} %copy.12.refs_0_, ...), custom_call_target="tpu_custom_call" | custom-call | flops 2147483648 | bytes 7898120 | tf_op jit(solution)/shard_map/negative_sums/pallas_call | solution.py:140
  94.2 3.7 %collective-permute-done.10.refs_5_ = bf16[256,512]{1,0:T(8,128)(2,1)S(1)} collective-permute-done((bf16[256,512]{1,0:T(8,128)(2,1)S(1)}, bf16[256,512]{1,0:T(8,128)(2,1)S(1)}, u32[]{:S(2)}, u32[]{:S(2)}) %collective-permute-start.10) | collective-permute-done | bytes 262176 | tf_op jit(solution)/shard_map/ppermute | solution.py:562
  97.9 5.7 %backward.1 = (bf16[1024,512]{1,0:T(8,128)(2,1)S(1)}, bf16[256,2560]{1,0:T(8,128)(2,1)S(1)}, bf16[256,2560]{1,0:T(8,128)(2,1)}) custom-call(s32[1]{0:T(128)S(6)} %copy.12.refs_0_, s32[4]{0:T(128)S(1)} %pad_add_fusion.refs_1_.refs_0_, f32[256,1]{1,0:T(8,128)S(1)} %get-tuple-element.67.refs_2_, f32[256,512]{1,0:T(8,128)S(1)} %get-tuple-element.55.refs_5_.refs_9_.refs_3_, ...), custom_call_target="tpu_custom_call" | custom-call | flops 1879048192 | bytes 11012116 | tf_op jit(solution)/shard_map/backward/pallas_call | solution.py:140
  107.2 7.4 %all-to-all-start.2 = ((bf16[128,8,512]{2,1,0:T(8,128)(2,1)}), bf16[128,8,512]{2,1,0:T(8,128)(2,1)S(1)}, u32[]{:S(2)}, u32[]{:S(2)}) async-start(bf16[128,8,512]{2,1,0:T(8,128)(2,1)} %bitcast.17), calls=%async_computation.2 | async-start | bytes 2097152 | tf_op jit(solution)/shard_map/all_to_all | solution.py:752
  114.6 2.7 %collective-permute-start.16 = (bf16[2,512,256]{2,1,0:T(8,128)(2,1)}, bf16[2,512,256]{2,1,0:T(8,128)(2,1)S(1)}, u32[]{:S(2)}, u32[]{:S(2)}) collective-permute-start(bf16[2,512,256]{2,1,0:T(8,128)(2,1)} %get-tuple-element.79), channel_id=1, source_target_pairs={{0,3},{1,2},{2,1},{3,0},{4,7},{5,6},{6,5},{7,4},{8,11},{9,10},{10,... | collective-permute-start | bytes 1572872 | tf_op jit(solution)/shard_map/ppermute | solution.py:555
  123.2 2.9 %collective-permute-start.14 = (bf16[64,2560]{1,0:T(8,128)(2,1)S(1)}, bf16[64,2560]{1,0:T(8,128)(2,1)S(1)}, u32[]{:S(2)}, u32[]{:S(2)}) collective-permute-start(bf16[64,2560]{1,0:T(8,128)(2,1)S(1)} %get-tuple-element.77), channel_id=1, source_target_pairs={{0,64},{16,80},{32,96},{48,112},{64,0},{80,16},{96,32},{112,48},{1... | collective-permute-start | bytes 983048 | tf_op jit(solution)/shard_map/ppermute | solution.py:546
  127.1 12.7 %collective-permute-done.16.refs_5_.refs_1_.first_ref = bf16[2,512,256]{2,1,0:T(8,128)(2,1)S(1)} collective-permute-done((bf16[2,512,256]{2,1,0:T(8,128)(2,1)}, bf16[2,512,256]{2,1,0:T(8,128)(2,1)S(1)}, u32[]{:S(2)}, u32[]{:S(2)}) %collective-permute-start.16) | collective-permute-done | bytes 524320 | tf_op jit(solution)/shard_map/ppermute | solution.py:555
  156.6 3.4 %collective-permute-done.22.refs_2_ = bf16[16,2560]{1,0:T(8,128)(2,1)S(1)} collective-permute-done((bf16[16,2560]{1,0:T(8,128)(2,1)S(1)}, bf16[16,2560]{1,0:T(8,128)(2,1)S(1)}, u32[]{:S(2)}, u32[]{:S(2)}) %collective-permute-start.22) | collective-permute-done | bytes 81952 | tf_op jit(solution)/shard_map/ppermute | solution.py:546
  176.8 5.4 %table_grad.1 = (f32[2048,512]{1,0:T(8,128)}, f32[8,128]{1,0:T(8,128)S(1)}) custom-call(s32[1,1024]{1,0:T(1,128)S(1)} %reshape.38.asked_ref, bf16[1024,512]{1,0:T(8,128)(2,1)S(1)} %bitcast.16, s32[1,512]{1,0:T(1,128)S(1)} %copy-done.35, bf16[512,512]{1,0:T(8,128)(2,1)S(1)} %copy-done.39, f32[512,512]{1,0:T(8,128)S(1)} %copy-done.37, ...), custom_call_target="tpu_custom_call" | custom-call | flops 3221225472 | bytes 4194304 | tf_op jit(solution)/shard_map/table_grad/pallas_call | solution.py:461
  182.2 4.0 %collective-permute-done.29.refs_1_ = bf16[4,16,2560]{2,1,0:T(8,128)(2,1)S(1)} collective-permute-done((bf16[4,16,2560]{2,1,0:T(8,128)(2,1)S(1)}, bf16[4,16,2560]{2,1,0:T(8,128)(2,1)S(1)}, u32[]{:S(2)}, u32[]{:S(2)}) %collective-permute-start.29) | collective-permute-done | bytes 327712 | tf_op jit(solution)/shard_map/ppermute | solution.py:546
  186.3 2.8 %collective-permute-start.32 = (bf16[16,16,2560]{2,1,0:T(8,128)(2,1)S(1)}, bf16[16,16,2560]{2,1,0:T(8,128)(2,1)S(1)}, u32[]{:S(2)}, u32[]{:S(2)}) collective-permute-start(bf16[16,16,2560]{2,1,0:T(8,128)(2,1)S(1)} %stack.21.refs_1_), channel_id=1, source_target_pairs={{0,16},{16,0},{32,48},{48,32},{64,80},{80,64},{96,112},{112,96},{1... | collective-permute-start | bytes 3932168 | tf_op jit(solution)/shard_map/ppermute | solution.py:546
  189.1 2.7 %collective-permute-done.32.refs_2_ = bf16[16,16,2560]{2,1,0:T(8,128)(2,1)S(1)} collective-permute-done((bf16[16,16,2560]{2,1,0:T(8,128)(2,1)S(1)}, bf16[16,16,2560]{2,1,0:T(8,128)(2,1)S(1)}, u32[]{:S(2)}, u32[]{:S(2)}) %collective-permute-start.32) | collective-permute-done | bytes 1310752 | tf_op jit(solution)/shard_map/ppermute | solution.py:546
  191.7 3.2 %place.1 = (f32[512,2048]{1,0:T(8,128)}, f32[512,512]{1,0:T(8,128)}) custom-call(s32[4]{0:T(128)S(1)} %pad_add_fusion.refs_1_.refs_0_, bf16[16,16,2560]{2,1,0:T(8,128)(2,1)S(1)} %stack.21.refs_1_, bf16[16,16,2560]{2,1,0:T(8,128)(2,1)S(1)} %collective-permute-done.32.refs_2_), custom_call_target="tpu_custom_call" | custom-call | bytes 7864336 | tf_op jit(solution)/shard_map/place/pallas_call | solution.py:140
  (151 shorter events, 69.5 us)
Async XLA Ops:
  5.3 22.7 %collective-permute-start.1 = (bf16[512,512]{1,0:T(8,128)(2,1)S(1)}, bf16[512,512]{1,0:T(8,128)(2,1)S(1)}, u32[]{:S(2)}, u32[]{:S(2)}) collective-permute-start(bf16[512,512]{1,0:T(8,128)(2,1)S(1)} %get-tuple-element.50.refs_2_.refs_1_), channel_id=1, source_target_pairs={{0,12},{1,13},{2,14},{3,15},{4,8},{5,9},{6,10},{7,11},{8,4},{9,5},... | collective-permute-start | bytes 1572872 | tf_op jit(solution)/shard_map/ppermute | solution.py:562
  8.9 19.1 %collective-permute-start = (bf16[512,512]{1,0:T(8,128)(2,1)S(1)}, bf16[512,512]{1,0:T(8,128)(2,1)S(1)}, u32[]{:S(2)}, u32[]{:S(2)}) collective-permute-start(bf16[512,512]{1,0:T(8,128)(2,1)S(1)} %get-tuple-element.50.refs_2_.refs_1_), channel_id=1, source_target_pairs={{0,3},{1,2},{2,1},{3,0},{4,7},{5,6},{6,5},{7,4},{8,11},{9,10},{10,... | collective-permute-start | bytes 1572872 | tf_op jit(solution)/shard_map/ppermute | solution.py:562
  32.2 26.4 %all-to-all-start.1 = ((bf16[128,8,512]{2,1,0:T(8,128)(2,1)}), bf16[128,8,512]{2,1,0:T(8,128)(2,1)S(1)}, u32[]{:S(2)}, u32[]{:S(2)}) async-start(bf16[128,8,512]{2,1,0:T(8,128)(2,1)} %bitcast.19), calls=%async_computation.1 | async-start | bytes 2097152 | tf_op jit(solution)/shard_map/all_to_all | solution.py:652
  39.6 27.5 %collective-permute-start.3 = (bf16[512,512]{1,0:T(8,128)(2,1)}, bf16[512,512]{1,0:T(8,128)(2,1)}, u32[]{:S(2)}, u32[]{:S(2)}) collective-permute-start(bf16[512,512]{1,0:T(8,128)(2,1)} %copy-done.5), channel_id=1, source_target_pairs={{0,15},{1,14},{2,13},{3,12},{4,11},{5,10},{6,9},{7,8},{8,7},{9,6},... | collective-permute-start | bytes 1572872 | tf_op jit(solution)/shard_map/ppermute | solution.py:562
  63.8 9.2 %collective-permute-start.5 = (bf16[256,512]{1,0:T(8,128)(2,1)}, bf16[256,512]{1,0:T(8,128)(2,1)S(1)}, u32[]{:S(2)}, u32[]{:S(2)}) collective-permute-start(bf16[256,512]{1,0:T(8,128)(2,1)} %get-tuple-element.53.refs_0_.refs_5_), channel_id=1, source_target_pairs={{0,4},{1,5},{2,6},{3,7},{4,0},{5,1},{6,2},{7,3},{8,12},{9,13},{10,... | collective-permute-start | bytes 786440 | tf_op jit(solution)/shard_map/ppermute | solution.py:562
  64.6 11.8 %collective-permute-start.4 = (bf16[256,512]{1,0:T(8,128)(2,1)}, bf16[256,512]{1,0:T(8,128)(2,1)}, u32[]{:S(2)}, u32[]{:S(2)}) collective-permute-start(bf16[256,512]{1,0:T(8,128)(2,1)} %get-tuple-element.53.refs_0_.refs_5_), channel_id=1, source_target_pairs={{0,1},{1,0},{2,3},{3,2},{4,5},{5,4},{6,7},{7,6},{8,9},{9,8},{10,11... | collective-permute-start | bytes 786440 | tf_op jit(solution)/shard_map/ppermute | solution.py:562
  64.9 14.4 %collective-permute-start.2 = (bf16[256,512]{1,0:T(8,128)(2,1)}, bf16[256,512]{1,0:T(8,128)(2,1)S(1)}, u32[]{:S(2)}, u32[]{:S(2)}) collective-permute-start(bf16[256,512]{1,0:T(8,128)(2,1)} %get-tuple-element.53.refs_0_.refs_5_), channel_id=1, source_target_pairs={{0,5},{1,4},{2,7},{3,6},{4,1},{5,0},{6,3},{7,2},{8,13},{9,12},{10,... | collective-permute-start | bytes 786440 | tf_op jit(solution)/shard_map/ppermute | solution.py:562
  82.3 7.2 %collective-permute-start.7 = (f32[8,256]{1,0:T(8,128)S(1)}, f32[8,256]{1,0:T(8,128)S(1)}, u32[]{:S(2)}, u32[]{:S(2)}) collective-permute-start(f32[8,256]{1,0:T(8,128)S(1)} %get-tuple-element.59.refs_4_.refs_1_), channel_id=1, source_target_pairs={{0,4},{1,5},{2,6},{3,7},{4,0},{5,1},{6,2},{7,3},{8,12},{9,13},{10,... | collective-permute-start | bytes 24584 | tf_op jit(solution)/shard_map/ppermute | solution.py:562
  83.4 6.1 %collective-permute-start.6 = (f32[8,256]{1,0:T(8,128)S(1)}, f32[8,256]{1,0:T(8,128)S(1)}, u32[]{:S(2)}, u32[]{:S(2)}) collective-permute-start(f32[8,256]{1,0:T(8,128)S(1)} %get-tuple-element.59.refs_4_.refs_1_), channel_id=1, source_target_pairs={{0,1},{1,0},{2,3},{3,2},{4,5},{5,4},{6,7},{7,6},{8,9},{9,8},{10,11... | collective-permute-start | bytes 24584 | tf_op jit(solution)/shard_map/ppermute | solution.py:562
  84.8 13.1 %collective-permute-start.10 = (bf16[256,512]{1,0:T(8,128)(2,1)S(1)}, bf16[256,512]{1,0:T(8,128)(2,1)S(1)}, u32[]{:S(2)}, u32[]{:S(2)}) collective-permute-start(bf16[256,512]{1,0:T(8,128)(2,1)S(1)} %get-tuple-element.69), channel_id=1, source_target_pairs={{0,4},{1,5},{2,6},{3,7},{4,0},{5,1},{6,2},{7,3},{8,12},{9,13},{10,... | collective-permute-start | bytes 786440 | tf_op jit(solution)/shard_map/ppermute | solution.py:562
  84.9 13.0 %collective-permute-start.11 = (bf16[256,512]{1,0:T(8,128)(2,1)S(1)}, bf16[256,512]{1,0:T(8,128)(2,1)S(1)}, u32[]{:S(2)}, u32[]{:S(2)}) collective-permute-start(bf16[256,512]{1,0:T(8,128)(2,1)S(1)} %get-tuple-element.70), channel_id=1, source_target_pairs={{0,5},{1,4},{2,7},{3,6},{4,1},{5,0},{6,3},{7,2},{8,13},{9,12},{10,... | collective-permute-start | bytes 786440 | tf_op jit(solution)/shard_map/ppermute | solution.py:562
  86.1 11.8 %collective-permute-start.9 = (bf16[256,512]{1,0:T(8,128)(2,1)S(1)}, bf16[256,512]{1,0:T(8,128)(2,1)S(1)}, u32[]{:S(2)}, u32[]{:S(2)}) collective-permute-start(bf16[256,512]{1,0:T(8,128)(2,1)S(1)} %get-tuple-element.68), channel_id=1, source_target_pairs={{0,1},{1,0},{2,3},{3,2},{4,5},{5,4},{6,7},{7,6},{8,9},{9,8},{10,11... | collective-permute-start | bytes 786440 | tf_op jit(solution)/shard_map/ppermute | solution.py:562
  104.6 15.1 %collective-permute-start.12 = (bf16[256,2560]{1,0:T(8,128)(2,1)}, bf16[256,2560]{1,0:T(8,128)(2,1)}, u32[]{:S(2)}, u32[]{:S(2)}) collective-permute-start(bf16[256,2560]{1,0:T(8,128)(2,1)} %get-tuple-element.74), channel_id=1, source_target_pairs={{0,16},{16,0},{32,48},{48,32},{64,80},{80,64},{96,112},{112,96},{1... | collective-permute-start | bytes 3932168 | tf_op jit(solution)/shard_map/ppermute | solution.py:546
  107.2 49.4 %all-to-all-start.2 = ((bf16[128,8,512]{2,1,0:T(8,128)(2,1)}), bf16[128,8,512]{2,1,0:T(8,128)(2,1)S(1)}, u32[]{:S(2)}, u32[]{:S(2)}) async-start(bf16[128,8,512]{2,1,0:T(8,128)(2,1)} %bitcast.17), calls=%async_computation.2 | async-start | bytes 2097152 | tf_op jit(solution)/shard_map/all_to_all | solution.py:752
  114.6 25.2 %collective-permute-start.16 = (bf16[2,512,256]{2,1,0:T(8,128)(2,1)}, bf16[2,512,256]{2,1,0:T(8,128)(2,1)S(1)}, u32[]{:S(2)}, u32[]{:S(2)}) collective-permute-start(bf16[2,512,256]{2,1,0:T(8,128)(2,1)} %get-tuple-element.79), channel_id=1, source_target_pairs={{0,3},{1,2},{2,1},{3,0},{4,7},{5,6},{6,5},{7,4},{8,11},{9,10},{10,... | collective-permute-start | bytes 1572872 | tf_op jit(solution)/shard_map/ppermute | solution.py:555
  117.3 22.9 %collective-permute-start.17 = (bf16[2,512,256]{2,1,0:T(8,128)(2,1)}, bf16[2,512,256]{2,1,0:T(8,128)(2,1)S(1)}, u32[]{:S(2)}, u32[]{:S(2)}) collective-permute-start(bf16[2,512,256]{2,1,0:T(8,128)(2,1)} %copy-done.31), channel_id=1, source_target_pairs={{0,12},{1,13},{2,14},{3,15},{4,8},{5,9},{6,10},{7,11},{8,4},{9,5},... | collective-permute-start | bytes 1572872 | tf_op jit(solution)/shard_map/ppermute | solution.py:555
  121.7 21.2 %collective-permute-start.13 = (bf16[64,2560]{1,0:T(8,128)(2,1)S(1)}, bf16[64,2560]{1,0:T(8,128)(2,1)S(1)}, u32[]{:S(2)}, u32[]{:S(2)}) collective-permute-start(bf16[64,2560]{1,0:T(8,128)(2,1)S(1)} %get-tuple-element.76), channel_id=1, source_target_pairs={{0,32},{16,48},{32,64},{48,80},{64,96},{80,112},{96,0},{112,16},{1... | collective-permute-start | bytes 983048 | tf_op jit(solution)/shard_map/ppermute | solution.py:546
  123.2 22.0 %collective-permute-start.14 = (bf16[64,2560]{1,0:T(8,128)(2,1)S(1)}, bf16[64,2560]{1,0:T(8,128)(2,1)S(1)}, u32[]{:S(2)}, u32[]{:S(2)}) collective-permute-start(bf16[64,2560]{1,0:T(8,128)(2,1)S(1)} %get-tuple-element.77), channel_id=1, source_target_pairs={{0,64},{16,80},{32,96},{48,112},{64,0},{80,16},{96,32},{112,48},{1... | collective-permute-start | bytes 983048 | tf_op jit(solution)/shard_map/ppermute | solution.py:546
  126.2 19.1 %collective-permute-start.15 = (bf16[64,2560]{1,0:T(8,128)(2,1)S(1)}, bf16[64,2560]{1,0:T(8,128)(2,1)S(1)}, u32[]{:S(2)}, u32[]{:S(2)}) collective-permute-start(bf16[64,2560]{1,0:T(8,128)(2,1)S(1)} %get-tuple-element.78), channel_id=1, source_target_pairs={{0,96},{16,112},{32,0},{48,16},{64,32},{80,48},{96,64},{112,80},{1... | collective-permute-start | bytes 983048 | tf_op jit(solution)/shard_map/ppermute | solution.py:546
  140.3 16.2 %collective-permute-start.24 = (bf16[512,256]{1,0:T(8,128)(2,1)S(1)}, bf16[512,256]{1,0:T(8,128)(2,1)S(1)}, u32[]{:S(2)}, u32[]{:S(2)}) collective-permute-start(bf16[512,256]{1,0:T(8,128)(2,1)S(1)} %get-tuple-element.87), channel_id=1, source_target_pairs={{0,12},{1,13},{2,14},{3,15},{4,8},{5,9},{6,10},{7,11},{8,4},{9,5},... | collective-permute-start | bytes 786440 | tf_op jit(solution)/shard_map/ppermute | solution.py:555
  142.5 14.0 %collective-permute-start.25 = (bf16[512,256]{1,0:T(8,128)(2,1)S(1)}, bf16[512,256]{1,0:T(8,128)(2,1)S(1)}, u32[]{:S(2)}, u32[]{:S(2)}) collective-permute-start(bf16[512,256]{1,0:T(8,128)(2,1)S(1)} %get-tuple-element.88), channel_id=1, source_target_pairs={{0,3},{1,2},{2,1},{3,0},{4,7},{5,6},{6,5},{7,4},{8,11},{9,10},{10,... | collective-permute-start | bytes 786440 | tf_op jit(solution)/shard_map/ppermute | solution.py:555
  169.0 13.1 %collective-permute-start.31 = (bf16[4,16,2560]{2,1,0:T(8,128)(2,1)S(1)}, bf16[4,16,2560]{2,1,0:T(8,128)(2,1)S(1)}, u32[]{:S(2)}, u32[]{:S(2)}) collective-permute-start(bf16[4,16,2560]{2,1,0:T(8,128)(2,1)S(1)} %pad_maximum_fusion.refs_0_), channel_id=1, source_target_pairs={{0,96},{16,112},{32,0},{48,16},{64,32},{80,48},{96,64},{112,80},{1... | collective-permute-start | bytes 983048 | tf_op jit(solution)/shard_map/ppermute | solution.py:546
  170.2 12.0 %collective-permute-start.30 = (bf16[4,16,2560]{2,1,0:T(8,128)(2,1)S(1)}, bf16[4,16,2560]{2,1,0:T(8,128)(2,1)S(1)}, u32[]{:S(2)}, u32[]{:S(2)}) collective-permute-start(bf16[4,16,2560]{2,1,0:T(8,128)(2,1)S(1)} %pad_maximum_fusion.refs_0_), channel_id=1, source_target_pairs={{0,64},{16,80},{32,96},{48,112},{64,0},{80,16},{96,32},{112,48},{1... | collective-permute-start | bytes 983048 | tf_op jit(solution)/shard_map/ppermute | solution.py:546
  171.2 15.0 %collective-permute-start.29 = (bf16[4,16,2560]{2,1,0:T(8,128)(2,1)S(1)}, bf16[4,16,2560]{2,1,0:T(8,128)(2,1)S(1)}, u32[]{:S(2)}, u32[]{:S(2)}) collective-permute-start(bf16[4,16,2560]{2,1,0:T(8,128)(2,1)S(1)} %pad_maximum_fusion.refs_0_), channel_id=1, source_target_pairs={{0,32},{16,48},{32,64},{48,80},{64,96},{80,112},{96,0},{112,16},{1... | collective-permute-start | bytes 983048 | tf_op jit(solution)/shard_map/ppermute | solution.py:546
  (51 other events, 391.8 us)
